TPU v7x, 512 devices: a whole 4x8x8 slice. The times are simulated.
512 devices in a mesh: dom: 64 (over x, z, core), sub: 8 (over y).
Axes of the slice: x: 4, y: 8, z: 8, core: 2. Of those that a mesh axis runs over, the one named last changes fastest.
Arguments:
- a_blocks: bfloat16 [8192, 7, 128, 128], P(('dom', 'sub')), may hold values from -6 to 6
- p_blocks: bfloat16 [8192, 128, 128], P(('dom', 'sub')), may hold values from -0.5 to 0.5
- a_cols: int32 [8192, 7], P(('dom', 'sub')), may hold values from 0 to 8191, as said below
- a_target: int32 [8192, 7], P(('dom', 'sub')), may hold values from 0 to 6
- agg: int32 [8192], P(('dom', 'sub')), may hold values from 0 to 2047, as said below
- refine: int32 [8192], P(('dom', 'sub')), may hold values from 0 to 1, as said below
Outputs:
- coarse_blocks: bfloat16 [2048, 7, 128, 128], P(('dom', 'sub'))
Inputs may be any that keep to these rules, and one draw needn't show every extreme that they name: a_cols[i, 0] = i, and every entry lies within 16 of its row index i. Fine row i, the r-th of device d = i // 16, has agg[i] = d * 4 + r // 4, except that one of the first 2 rows of a device may name d * 4 - 1 and one of the last 2 may name (d + 1) * 4. `refine`: at most 8 rows of one device are marked, and some device has exactly 8.
All inputs are finite; a program needn't handle non-finite values.
Results may differ from a plain program's by a relative error of at most 0.0049.
Values may be sent and summed in bfloat16 or wider, within the bound.
No kernel may reach another device: no remote copies, remote signals or barrier semaphores. Data moves between devices by JAX's collectives and lax.ppermute only.
A program may use at most 64 MiB of HBM per device.

v0:
```python
import jax
import jax.numpy as jnp
from jax import lax
from jax.sharding import PartitionSpec as P

SLOTS_COARSE = 7
ALWAYS_LIVE = 3
AGG_SIZE = 4


def extended_2(block, sides, width):
    for axis, dim in sides:
        count = lax.axis_size(axis)
        forward = [(i, i + 1) for i in range(count - 1)]
        backward = [(target, source) for source, target in forward]
        low = lax.ppermute(
            lax.slice_in_dim(block, block.shape[dim] - width, None, axis=dim), axis, forward
        )
        high = lax.ppermute(lax.slice_in_dim(block, 0, width, axis=dim), axis, backward)
        block = jnp.concatenate([low, block, high], axis=dim)
    return block


def passed_along(block, axis, distance):
    devices = range(lax.axis_size(axis))
    route = [(i - distance, i) for i in devices if i - distance in devices]
    return lax.ppermute(block, axis, route)


def body(a_blocks, p_blocks, a_cols, a_target, agg, refine):
    row_count = a_blocks.shape[0]
    slot_count = a_blocks.shape[1]
    block_dim = a_blocks.shape[2]
    coarse_count = row_count // AGG_SIZE
    coarse_slots = SLOTS_COARSE
    device = lax.axis_index(("dom", "sub"))
    first_row = device * row_count
    first_coarse = device * coarse_count
    extended = extended_2(p_blocks, ((("dom", "sub"), 0),), row_count)
    flat_count = row_count * slot_count
    live_mask = ((jnp.arange(slot_count)[None, :] < ALWAYS_LIVE) | (refine[:, None] == 1)).reshape(
        -1
    )
    row_of = jnp.broadcast_to(
        jnp.arange(row_count, dtype=jnp.int32)[:, None], (row_count, slot_count)
    ).reshape(-1)
    col_of = (a_cols - first_row + row_count).reshape(-1)
    target_of = a_target.reshape(-1)
    block_list = a_blocks.reshape(flat_count, block_dim, block_dim)
    ghost_blocks = extended[col_of]
    products = jnp.einsum(
        "nij,njc->nic", block_list, ghost_blocks, preferred_element_type=jnp.float32
    ).astype(jnp.bfloat16)
    contrib = jnp.einsum(
        "nfb,nfc->nbc", p_blocks[row_of], products, preferred_element_type=jnp.float32
    )
    item_coarse = agg[row_of] - first_coarse
    own_total = coarse_count * coarse_slots
    inside = live_mask & (item_coarse >= -coarse_count) & (item_coarse < 2 * coarse_count)
    segment = jnp.where(
        inside, (item_coarse + coarse_count) * coarse_slots + target_of, 3 * own_total
    )
    partial_value = jax.ops.segment_sum(contrib, segment, num_segments=3 * own_total + 1)[:-1]
    partial_value = partial_value.reshape(3, own_total, block_dim, block_dim)
    from_next = passed_along(partial_value[0], ("dom", "sub"), -1)
    from_prev = passed_along(partial_value[2], ("dom", "sub"), 1)
    result = partial_value[1] + from_next + from_prev
    return result.reshape(coarse_count, coarse_slots, block_dim, block_dim).astype(jnp.bfloat16)


def solution(mesh):
    return jax.shard_map(
        body,
        mesh=mesh,
        in_specs=(
            P(("dom", "sub"), None, None, None),
            P(("dom", "sub"), None, None),
            P(("dom", "sub"), None),
            P(("dom", "sub"), None),
            P(("dom", "sub")),
            P(("dom", "sub")),
        ),
        out_specs=P(("dom", "sub"), None, None, None),
        check_vma=False,
    )
```

profile of v0, /device:TPU:6, one launch (start us, length us, event | category | flops | bytes accessed | tf_op | source)
XLA Modules:
  0.0 129.9 jit_solution(14383133277723633023)
XLA Ops:
  0.0 3.5 %collective-permute-start = (bf16[16,128,128]{2,1,0:T(8,128)(2,1)}, bf16[16,128,128]{2,1,0:T(8,128)(2,1)S(1)}, u32[]{:S(2)}, u32[]{:S(2)}) collective-permute-start(bf16[16,128,128]{2,1,0:T(8,128)(2,1)} %param.7), channel_id=1, source_target_pairs={{0,1},{1,2},{2,3},{3,4},{4,5},{5,6},{6,7},{7,8},{8,9},{9,10},{10,1... | collective-permute-start | bytes 1572872 | tf_op jit(solution)/shard_map/ppermute | solution.py:16
  3.5 12.0 %collective-permute-start.1 = (bf16[16,128,128]{2,1,0:T(8,128)(2,1)}, bf16[16,128,128]{2,1,0:T(8,128)(2,1)S(1)}, u32[]{:S(2)}, u32[]{:S(2)}) collective-permute-start(bf16[16,128,128]{2,1,0:T(8,128)(2,1)} %param.7), channel_id=1, source_target_pairs={{1,0},{2,1},{3,2},{4,3},{5,4},{6,5},{7,6},{8,7},{9,8},{10,9},{11,1... | collective-permute-start | bytes 1572872 | tf_op jit(solution)/shard_map/ppermute | solution.py:19
  15.5 0.7 broadcast_compare_fusion
  16.2 0.1 broadcast_or_fusion
  16.2 0.1 or.27
  16.3 0.7 subtract_add_fusion
  17.0 0.1 copy.11
  17.1 0.1 reshape.157
  17.2 0.8 copy.10
  18.0 0.1 reshape.156
  18.1 0.1 reshape.155
  18.2 0.0 copy-start.1
  18.2 0.0 copy-start
  18.2 4.1 %gather_fusion = bf16[112,128,128]{2,1,0:T(8,128)(2,1)} fusion(bf16[16,128,128]{2,1,0:T(8,128)(2,1)} %param.7, s32[1024]{0:T(1024)S(1)} %pad_clamp_fusion.1), kind=kCustom, calls=%fused_computation | custom fusion | bytes 7340480 | tf_op jit(solution)/shard_map/gather | solution.py:55
  22.3 0.0 copy-done.1
  22.3 0.7 fusion.12
  23.1 10.0 %fusion.10 = s32[112]{0:T(128)S(1)} fusion(s32[112,1]{0,1:T(1,128)S(1)} %reshape.156, pred[112,1]{0,1:T(4,128)(4,1)S(1)} %or.27, s32[]{:T(128)} %bitcast.1, s32[]{:T(128)} %bitcast.2, s32[]{:T(128)} %bitcast.3, s32[]{:T(128)} %bitcast.4, s32[]{:T(128)} %bitcast.5, s32[]{:T(128)} %bitcast.6, s32[]{:T(128)} %bitcast.7, s32[]{:T(128)} %bitcast.8, s32[]{:T(128)} %bitcast.9, ...), kind=kLoop, calls=%fused_computation.39 | loop fusion | flops 4704 | bytes 1524 | tf_op jit(solution)/shard_map/jit(_where)/select_n | solution.py:60
  33.1 0.0 collective-permute-done
  33.1 0.0 collective-permute-done.1
  33.1 0.0 copy-done
  33.1 0.2 pad_maximum_fusion
  33.3 3.0 %gather_fusion.1 = bf16[112,128,128]{2,1,0:T(8,128)(2,1)} fusion(bf16[48,128,128]{2,1,0:T(8,128)(2,1)S(1)} %pad_maximum_fusion, s32[1024]{0:T(1024)S(1)} %pad_clamp_fusion), kind=kCustom, calls=%fused_computation.1 | custom fusion | bytes 7340480 | tf_op jit(solution)/shard_map/gather | solution.py:50
  36.3 12.4 %fusion = f32[112,128,128]{2,1,0:T(8,128)} fusion(bf16[112,128,128]{2,1,0:T(8,128)(2,1)} %gather_fusion, bf16[112,128,128]{2,1,0:T(8,128)(2,1)} %gather_fusion.1, bf16[112,128,128]{2,1,0:T(8,128)(2,1)} %bitcast.47), kind=kOutput, calls=%fused_computation.3 | convolution fusion | flops 941359104 | bytes 18350080 | tf_op jit(solution)/shard_map/nfb,nfc->nbc/dot_general | solution.py:54
  48.7 3.1 %broadcast_in_dim.9 = f32[85,128,128]{2,1,0:T(8,128)} broadcast(f32[]{:T(128)} %constant.14.clone.1), dimensions={} | broadcast | bytes 5570564 | tf_op jit(solution)/shard_map/broadcast_in_dim | solution.py:63
  51.7 22.6 %scatter_fusion = f32[85,128,128]{2,1,0:T(8,128)} fusion(f32[85,128,128]{2,1,0:T(8,128)} %broadcast_in_dim.9, s32[112]{0:T(128)S(1)} %fusion.10, f32[112,128,128]{2,1,0:T(8,128)} %fusion), kind=kCustom, calls=%fused_computation.2 | custom fusion | flops 1835008 | bytes 22020544 | tf_op jit(solution)/shard_map/scatter-add | solution.py:63
  74.3 2.5 %fusion.11 = (f32[28,128,128]{2,1,0:T(8,128)S(1)}, f32[28,128,128]{2,1,0:T(8,128)S(1)}) fusion(f32[85,128,128]{2,1,0:T(8,128)} %scatter_fusion), kind=kLoop, calls=%fused_computation.41 | loop fusion | bytes 7340032 | tf_op jit(solution)/shard_map/slice | solution.py:65
  76.8 3.3 %collective-permute-start.2 = (f32[28,128,128]{2,1,0:T(8,128)S(1)}, f32[28,128,128]{2,1,0:T(8,128)S(1)}, u32[]{:S(2)}, u32[]{:S(2)}) collective-permute-start(f32[28,128,128]{2,1,0:T(8,128)S(1)} %get-tuple-element.5), channel_id=1, source_target_pairs={{1,0},{2,1},{3,2},{4,3},{5,4},{6,5},{7,6},{8,7},{9,8},{10,9},{11,1... | collective-permute-start | bytes 5505032 | tf_op jit(solution)/shard_map/ppermute | solution.py:27
  80.1 2.6 %collective-permute-start.3 = (f32[28,128,128]{2,1,0:T(8,128)S(1)}, f32[28,128,128]{2,1,0:T(8,128)S(1)}, u32[]{:S(2)}, u32[]{:S(2)}) collective-permute-start(f32[28,128,128]{2,1,0:T(8,128)S(1)} %get-tuple-element.6), channel_id=1, source_target_pairs={{0,1},{1,2},{2,3},{3,4},{4,5},{5,6},{6,7},{7,8},{8,9},{9,10},{10,1... | collective-permute-start | bytes 5505032 | tf_op jit(solution)/shard_map/ppermute | solution.py:27
  82.6 29.9 %collective-permute-done.2 = f32[28,128,128]{2,1,0:T(8,128)S(1)} collective-permute-done((f32[28,128,128]{2,1,0:T(8,128)S(1)}, f32[28,128,128]{2,1,0:T(8,128)S(1)}, u32[]{:S(2)}, u32[]{:S(2)}) %collective-permute-start.2) | collective-permute-done | bytes 1835040 | tf_op jit(solution)/shard_map/ppermute | solution.py:27
  112.5 14.5 %collective-permute-done.3 = f32[28,128,128]{2,1,0:T(8,128)S(1)} collective-permute-done((f32[28,128,128]{2,1,0:T(8,128)S(1)}, f32[28,128,128]{2,1,0:T(8,128)S(1)}, u32[]{:S(2)}, u32[]{:S(2)}) %collective-permute-start.3) | collective-permute-done | bytes 1835040 | tf_op jit(solution)/shard_map/ppermute | solution.py:27
  127.0 3.0 %fusion.5 = bf16[28,128,128]{2,1,0:T(8,128)(2,1)} fusion(f32[28,128,128]{2,1,0:T(8,128)S(1)} %collective-permute-done.3, f32[28,128,128]{2,1,0:T(8,128)S(1)} %collective-permute-done.2, f32[85,128,128]{2,1,0:T(8,128)} %scatter_fusion), kind=kLoop, calls=%fused_computation.8 | loop fusion | flops 1376256 | bytes 6422528 | tf_op jit(solution)/shard_map/convert_element_type | solution.py:68
  (6 shorter events, 0.0 us)
Async XLA Ops:
  0.0 33.1 %collective-permute-start = (bf16[16,128,128]{2,1,0:T(8,128)(2,1)}, bf16[16,128,128]{2,1,0:T(8,128)(2,1)S(1)}, u32[]{:S(2)}, u32[]{:S(2)}) collective-permute-start(bf16[16,128,128]{2,1,0:T(8,128)(2,1)} %param.7), channel_id=1, source_target_pairs={{0,1},{1,2},{2,3},{3,4},{4,5},{5,6},{6,7},{7,8},{8,9},{9,10},{10,1... | collective-permute-start | bytes 1572872 | tf_op jit(solution)/shard_map/ppermute | solution.py:16
  3.5 29.6 %collective-permute-start.1 = (bf16[16,128,128]{2,1,0:T(8,128)(2,1)}, bf16[16,128,128]{2,1,0:T(8,128)(2,1)S(1)}, u32[]{:S(2)}, u32[]{:S(2)}) collective-permute-start(bf16[16,128,128]{2,1,0:T(8,128)(2,1)} %param.7), channel_id=1, source_target_pairs={{1,0},{2,1},{3,2},{4,3},{5,4},{6,5},{7,6},{8,7},{9,8},{10,9},{11,1... | collective-permute-start | bytes 1572872 | tf_op jit(solution)/shard_map/ppermute | solution.py:19
  18.2 4.1 %copy-start.1 = (s32[16]{0:T(128)S(1)}, s32[16]{0:T(128)}, u32[]{:S(2)}) copy-start(s32[16]{0:T(128)} %param.10) | copy-start | bytes 196
  18.2 14.9 %copy-start = (bf16[16,128,128]{2,1,0:T(8,128)(2,1)S(1)}, bf16[16,128,128]{2,1,0:T(8,128)(2,1)}, u32[]{:S(2)}) copy-start(bf16[16,128,128]{2,1,0:T(8,128)(2,1)} %param.7) | copy-start | bytes 1572868
  76.8 35.7 %collective-permute-start.2 = (f32[28,128,128]{2,1,0:T(8,128)S(1)}, f32[28,128,128]{2,1,0:T(8,128)S(1)}, u32[]{:S(2)}, u32[]{:S(2)}) collective-permute-start(f32[28,128,128]{2,1,0:T(8,128)S(1)} %get-tuple-element.5), channel_id=1, source_target_pairs={{1,0},{2,1},{3,2},{4,3},{5,4},{6,5},{7,6},{8,7},{9,8},{10,9},{11,1... | collective-permute-start | bytes 5505032 | tf_op jit(solution)/shard_map/ppermute | solution.py:27
  80.1 46.9 %collective-permute-start.3 = (f32[28,128,128]{2,1,0:T(8,128)S(1)}, f32[28,128,128]{2,1,0:T(8,128)S(1)}, u32[]{:S(2)}, u32[]{:S(2)}) collective-permute-start(f32[28,128,128]{2,1,0:T(8,128)S(1)} %get-tuple-element.6), channel_id=1, source_target_pairs={{0,1},{1,2},{2,3},{3,4},{4,5},{5,6},{6,7},{7,8},{8,9},{9,10},{10,1... | collective-permute-start | bytes 5505032 | tf_op jit(solution)/shard_map/ppermute | solution.py:27
where the time goes:
time: 131 us; the launch traced here: 130 us
  waiting for transfers between devices  44.3 us (34%)
  other arithmetic  37.2 us (28%)
  starting transfers between devices  21.3 us (16%)
  local copies, waits for them, and re-layouts  14.6 us (11%)
  matrix products  12.4 us (9%)
    ppermute x2, waiting for transfers between devices, passed_along(): return lax.ppermute(block, axis, route)  44.3 us
    scatter-add x1, other arithmetic, body(): jax.ops.segment_sum(contrib, segment, num_segments=3 * own_total + 1)[:-1]  22.6 us
    dot_general x1, matrix products, body(): jnp.einsum('nfb,nfc->nbc', p_blocks[row_of], products, preferred_element_...  12.4 us
    ppermute x1, starting transfers between devices, extended_2(): lax.ppermute(lax.slice_in_dim(block, 0, width, axis=dim), axis, backward)  12 us
    select_n x1, other arithmetic, body(): jnp.where(inside, (item_coarse + coarse_count) * coarse_slots + target_of...  10 us
    ppermute x2, starting transfers between devices, passed_along(): return lax.ppermute(block, axis, route)  5.84 us
    gather x1, local copies, waits for them, and re-layouts, body(): p_blocks[row_of]  4.09 us
    ppermute x1, starting transfers between devices, extended_2(): lax.ppermute(lax.slice_in_dim(block, block.shape[dim] - width, None, axis...  3.47 us
  transfers between devices with their start and end apart: 4, of which 2 were waited for; matrix products, arithmetic and copies ran while one was open for 13% of the time, Pallas kernels for 0%

commit v1 on v0

v1 whole, which is shorter than its diff:
```python
import jax
import jax.numpy as jnp
from jax import lax
from jax.experimental import pallas as pl
from jax.experimental.pallas import tpu as pltpu
from jax.sharding import PartitionSpec as P

ROWS = 16
DIM = 128
SLOTS = 7
LIVE = 3
COARSE = 4
SEGS = COARSE * SLOTS
DUMP = SEGS
UNROLL = 8
HALO_MAX = 64 + UNROLL
LIST = 128
MSG = SLOTS * DIM + 16
AXES = ("dom", "sub")
F32 = jnp.float32
BF16 = jnp.bfloat16

SMEM = pl.BlockSpec(memory_space=pltpu.SMEM)
VMEM = pl.BlockSpec(memory_space=pltpu.VMEM)
ANY = pl.BlockSpec(memory_space=pl.ANY)


def dot(x, y):
    return jnp.dot(x, y, preferred_element_type=F32)


def run_copies(copies):
    for copy in copies:
        copy.start()
    for copy in copies:
        copy.wait()


def moved_row(agg, first_row, up):
    first_coarse = first_row // COARSE
    low = agg[0] < first_coarse
    low_any = low | (agg[1] < first_coarse)
    high = agg[ROWS - 1] >= first_coarse + COARSE
    high_any = high | (agg[ROWS - 2] >= first_coarse + COARSE)
    row = jnp.where(up, jnp.where(high, ROWS - 1, ROWS - 2), jnp.where(low, 0, 1))
    return row, jnp.where(up, high_any, low_any)


def edge_kernel(cols, target, agg, refine, a, p, msg_a, msg_b, a_buf, p_buf, sems):
    first_row = cols[0, 0]
    odd = (first_row // ROWS) % 2 == 1
    picks = [moved_row(agg, first_row, odd), moved_row(agg, first_row, jnp.logical_not(odd))]
    copies = []
    for side, (row, _) in enumerate(picks):
        copies.append(pltpu.make_async_copy(p.at[row], p_buf.at[side], sems.at[2 * side]))
        copies.append(pltpu.make_async_copy(a.at[row], a_buf.at[side], sems.at[2 * side + 1]))
    for copy in copies:
        copy.start()
    lane = lax.broadcasted_iota(jnp.int32, (16, DIM), 1)
    for side, (row, found) in enumerate(picks):
        msg = (msg_a, msg_b)[side]
        up = odd if side == 0 else jnp.logical_not(odd)
        shift = jnp.where(up, 2 - ROWS, 2 + ROWS) + ROWS - first_row
        fine = refine[row] == 1
        note = jnp.zeros((16, DIM), F32)
        for k in range(SLOTS):
            live = found if k < LIVE else found & fine
            column = (cols[row, k] + shift).astype(F32)
            aim = jnp.where(live, target[row, k], SLOTS).astype(F32)
            note = jnp.where(lane == 2 * k, column, note)
            note = jnp.where(lane == 2 * k + 1, aim, note)
        msg[SLOTS * DIM : MSG, :] = note.astype(BF16)
    for side in range(2):
        msg = (msg_a, msg_b)[side]
        copies[2 * side].wait()
        copies[2 * side + 1].wait()
        turned = p_buf[side].T
        for k in range(SLOTS):
            msg[k * DIM : (k + 1) * DIM, :] = dot(turned, a_buf[side, k]).astype(BF16)


def add_items(count, codes, left, right, acc, by_slot):
    def step(at, carry):
        parts = []
        for j in range(UNROLL):
            n = at * UNROLL + j
            code = codes[n]
            slot = (code & 127) if by_slot else n
            parts.append((code >> 12, dot(left[slot], right[(code >> 7) & 31])))
        for seg, part in parts:
            acc[seg] += part
        return carry

    lax.fori_loop(0, (count + UNROLL - 1) // UNROLL, step, 0)


def own_kernel(cols, target, agg, refine, a, p, acc, left_halo, halo, halo_count, own, left):
    first_row = cols[0, 0]
    first_coarse = first_row // COARSE

    def listing(row, counts):
        own_n, halo_n = counts
        group = agg[row] - first_coarse
        inside = (group >= 0) & (group < COARSE)
        fine = inside & (refine[row] == 1)
        for k in range(SLOTS):
            live = inside if k < LIVE else fine
            column = cols[row, k] - first_row
            seg = group * SLOTS + target[row, k]
            here = (column >= 0) & (column < ROWS)
            slot = row * SLOTS + k
            entry = slot + seg * 4096
            place = jnp.where(column < 0, column + ROWS, column)
            own[own_n] = entry + (column & 15) * 128
            halo[halo_n] = entry + (place & 31) * 128
            own_n += (live & here).astype(jnp.int32)
            halo_n += (live & jnp.logical_not(here)).astype(jnp.int32)
        return own_n, halo_n

    own_n, halo_n = lax.fori_loop(0, ROWS, listing, (0, 0))
    for j in range(UNROLL):
        own[own_n + j] = DUMP * 4096
        halo[halo_n + j] = DUMP * 4096
    halo_count[0] = halo_n

    def multiply(row, carry):
        turned = p[row].T
        for k in range(LIVE):
            left[row * SLOTS + k] = dot(turned, a[row, k]).astype(BF16)

        @pl.when(refine[row] == 1)
        def _():
            for k in range(LIVE, SLOTS):
                left[row * SLOTS + k] = dot(turned, a[row, k]).astype(BF16)

        return carry

    lax.fori_loop(0, ROWS, multiply, 0)
    acc[...] = jnp.zeros(acc.shape, F32)
    add_items(own_n, own, left, p, acc, True)

    def keep(at, carry):
        for j in range(UNROLL):
            n = at * UNROLL + j
            left_halo[n] = left[halo[n] & 127]
        return carry

    lax.fori_loop(0, (halo_n + UNROLL - 1) // UNROLL, keep, 0)


def halo_kernel(cols, halo, halo_count, acc_in, left_halo, from_a, from_b, acc, table, sems):
    odd = (cols[0, 0] // ROWS) % 2
    copies = [
        pltpu.make_async_copy(from_a, table.at[pl.ds(odd * ROWS, ROWS)], sems.at[0]),
        pltpu.make_async_copy(from_b, table.at[pl.ds((1 - odd) * ROWS, ROWS)], sems.at[1]),
    ]
    for copy in copies:
        copy.start()
    acc[...] = acc_in[...]
    for copy in copies:
        copy.wait()
    add_items(halo_count[0], halo, left_halo, table, acc, False)


def last_kernel(cols, acc, msg_a, msg_b, p, from_a, from_b, before, after, out, table, rest, sems):
    odd = (cols[0, 0] // ROWS) % 2
    copies = [
        pltpu.make_async_copy(before, table.at[pl.ds(0, 2)], sems.at[0]),
        pltpu.make_async_copy(from_a, table.at[pl.ds(2 + odd * 2 * ROWS, ROWS)], sems.at[1]),
        pltpu.make_async_copy(p, table.at[pl.ds(2 + ROWS, ROWS)], sems.at[2]),
        pltpu.make_async_copy(from_b, table.at[pl.ds(2 + (1 - odd) * 2 * ROWS, ROWS)], sems.at[3]),
        pltpu.make_async_copy(after, table.at[pl.ds(2 + 3 * ROWS, 2)], sems.at[4]),
    ]
    for copy in copies:
        copy.start()
    lane = lax.broadcasted_iota(jnp.int32, (1, DIM), 1)
    scale = jnp.where(lane % 2 == 0, 1.0, 64.0)
    codes = []
    for msg in (msg_a, msg_b):
        note = msg[SLOTS * DIM : MSG, :].astype(F32)[0:1] * scale
        for k in range(SLOTS):
            codes.append(jnp.sum(jnp.where(lane // 2 == k, note, 0.0)).astype(jnp.int32))
    for copy in copies:
        copy.wait()
    rest[...] = jnp.zeros(rest.shape, F32)
    for side, msg in enumerate((msg_a, msg_b)):
        above = odd if side == 0 else 1 - odd
        parts = []
        for k in range(SLOTS):
            code = codes[side * SLOTS + k]
            aim = code >> 6
            seg = above * (SLOTS + 1) + aim
            parts.append((seg, dot(msg[k * DIM : (k + 1) * DIM, :], table[code & 63])))
        for seg, part in parts:
            rest[seg] += part
    for s in range(SEGS):
        value = acc[s]
        if s < SLOTS:
            value = value + rest[s]
        if s >= SEGS - SLOTS:
            value = value + rest[SLOTS + 1 + s - (SEGS - SLOTS)]
        out[s // SLOTS, s % SLOTS] = value.astype(BF16)


def call(kernel, ins, outs, out_specs, in_specs, scratch, cost, **more):
    return pl.pallas_call(
        kernel,
        out_shape=outs,
        in_specs=in_specs,
        out_specs=out_specs,
        scratch_shapes=scratch,
        cost_estimate=pl.CostEstimate(flops=cost[0], bytes_accessed=cost[1], transcendentals=0),
        compiler_params=pltpu.CompilerParams(vmem_limit_bytes=40 * 1024 * 1024),
        **more,
    )(*ins)


def body(a_blocks, p_blocks, a_cols, a_target, agg, refine):
    count = lax.axis_size(AXES)
    shape = jax.ShapeDtypeStruct
    odd_pairs = [(i, i + 1) for i in range(1, count - 1, 2)]
    even_pairs = [(i, i + 1) for i in range(0, count, 2)]
    pairs_a = odd_pairs + [(j, i) for i, j in odd_pairs]
    pairs_b = even_pairs + [(j, i) for i, j in even_pairs]
    two_up = [(i, i + 2) for i in range(count - 2)]
    two_down = [(j, i) for i, j in two_up]
    block_cost = 2 * DIM**3

    from_a = lax.ppermute(p_blocks, AXES, pairs_a)
    from_b = lax.ppermute(p_blocks, AXES, pairs_b)
    ints = (a_cols, a_target, agg, refine)
    msg_a, msg_b = call(
        edge_kernel,
        (*ints, a_blocks, p_blocks),
        [shape((MSG, DIM), BF16)] * 2,
        [VMEM] * 2,
        [SMEM] * 4 + [ANY] * 2,
        [
            pltpu.VMEM((2, SLOTS, DIM, DIM), BF16),
            pltpu.VMEM((2, DIM, DIM), BF16),
            pltpu.SemaphoreType.DMA((4,)),
        ],
        (14 * block_cost, 28 * 32768),
    )
    got_a = lax.ppermute(msg_a, AXES, pairs_a)
    got_b = lax.ppermute(msg_b, AXES, pairs_b)
    before = lax.ppermute(p_blocks[ROWS - 2 :], AXES, two_up)
    after = lax.ppermute(p_blocks[:2], AXES, two_down)
    acc, left_halo, halo, halo_count = call(
        own_kernel,
        (*ints, a_blocks, p_blocks),
        [
            shape((SEGS + 1, DIM, DIM), F32),
            shape((HALO_MAX, DIM, DIM), BF16),
            shape((LIST,), jnp.int32),
            shape((1,), jnp.int32),
        ],
        [VMEM, VMEM, SMEM, SMEM],
        [SMEM] * 4 + [VMEM] * 2,
        [pltpu.SMEM((LIST,), jnp.int32), pltpu.VMEM((ROWS * SLOTS, DIM, DIM), BF16)],
        (128 * block_cost, 8 << 20),
    )
    acc = call(
        halo_kernel,
        (a_cols, halo, halo_count, acc, left_halo, from_a, from_b),
        shape((SEGS + 1, DIM, DIM), F32),
        VMEM,
        [SMEM] * 3 + [VMEM] * 2 + [ANY] * 2,
        [pltpu.VMEM((2 * ROWS, DIM, DIM), BF16), pltpu.SemaphoreType.DMA((2,))],
        (32 * block_cost, 6 << 20),
    )
    return call(
        last_kernel,
        (a_cols, acc, got_a, got_b, p_blocks, from_a, from_b, before, after),
        shape((COARSE, SLOTS, DIM, DIM), BF16),
        VMEM,
        [SMEM] + [VMEM] * 3 + [ANY] * 5,
        [
            pltpu.VMEM((3 * ROWS + 4, DIM, DIM), BF16),
            pltpu.VMEM((2 * (SLOTS + 1), DIM, DIM), F32),
            pltpu.SemaphoreType.DMA((5,)),
        ],
        (14 * block_cost, 5 << 20),
    )


def solution(mesh):
    return jax.shard_map(
        body,
        mesh=mesh,
        in_specs=(
            P(AXES, None, None, None),
            P(AXES, None, None),
            P(AXES, None),
            P(AXES, None),
            P(AXES),
            P(AXES),
        ),
        out_specs=P(AXES, None, None, None),
        check_vma=False,
    )
```

time: 131 us -> 54.7 us (0.42)
  the two profiles are of different devices: /device:TPU:6 before, /device:TPU:10 now
where the time goes in v1:
time: 54.7 us; the launch traced here: 54.3 us
  starting transfers between devices  32.3 us (59%)
  Pallas kernels  15.9 us (29%)
  local copies, waits for them, and re-layouts  5.93 us (11%)
    pallas_call x4, Pallas kernels, call(): pl.pallas_call(kernel, out_shape=outs, in_specs=in_specs, out_specs=out_s...  15.9 us
    ppermute x1, starting transfers between devices, body(): from_b = lax.ppermute(p_blocks, AXES, pairs_b)  12.1 us
    ppermute x1, starting transfers between devices, body(): after = lax.ppermute(p_blocks[:2], AXES, two_down)  7.42 us
    unnamed x12, local copies, waits for them, and re-layouts  5.92 us
    ppermute x1, starting transfers between devices, body(): got_b = lax.ppermute(msg_b, AXES, pairs_b)  4.04 us
    ppermute x1, starting transfers between devices, body(): from_a = lax.ppermute(p_blocks, AXES, pairs_a)  3.47 us
    ppermute x1, starting transfers between devices, body(): before = lax.ppermute(p_blocks[ROWS - 2:], AXES, two_up)  3.26 us
    ppermute x1, starting transfers between devices, body(): got_a = lax.ppermute(msg_a, AXES, pairs_a)  1.92 us
  transfers between devices with their start and end apart: 6, of which 0 were waited for; matrix products, arithmetic and copies ran while one was open for 3% of the time, Pallas kernels for 25%

profile of v1, /device:TPU:10, one launch (start us, length us, event | category | flops | bytes accessed | tf_op | source)
XLA Modules:
  0.0 54.3 jit_solution(16375403487662074072)
XLA Ops:
  0.0 3.5 %collective-permute-start = (bf16[16,128,128]{2,1,0:T(8,128)(2,1)}, bf16[16,128,128]{2,1,0:T(8,128)(2,1)S(1)}, u32[]{:S(2)}, u32[]{:S(2)}) collective-permute-start(bf16[16,128,128]{2,1,0:T(8,128)(2,1)} %p.5), channel_id=1, source_target_pairs={{1,2},{3,4},{5,6},{7,8},{9,10},{11,12},{13,14},{15,16},{17,18},{19... | collective-permute-start | bytes 1572872 | tf_op jit(solution)/shard_map/ppermute | solution.py:229
  3.5 12.1 %collective-permute-start.1 = (bf16[16,128,128]{2,1,0:T(8,128)(2,1)}, bf16[16,128,128]{2,1,0:T(8,128)(2,1)S(1)}, u32[]{:S(2)}, u32[]{:S(2)}) collective-permute-start(bf16[16,128,128]{2,1,0:T(8,128)(2,1)} %p.5), channel_id=1, source_target_pairs={{0,1},{2,3},{4,5},{6,7},{8,9},{10,11},{12,13},{14,15},{16,17},{18,... | collective-permute-start | bytes 1572872 | tf_op jit(solution)/shard_map/ppermute | solution.py:230
  15.6 0.8 %copy.12.cols = s32[16,7]{1,0:T(8,128)S(1)} copy(s32[16,7]{0,1:T(8,128)} %param.8) | data formatting | bytes 896 | tf_op args[2]
  16.4 0.8 %copy.8.target = s32[16,7]{1,0:T(8,128)S(1)} copy(s32[16,7]{0,1:T(8,128)} %param.9) | data formatting | bytes 896 | tf_op args[3]
  17.2 0.0 copy-start
  17.2 2.0 %copy-done = bf16[16,7,128,128]{3,2,1,0:T(8,128)(2,1)S(1)} copy-done((bf16[16,7,128,128]{3,2,1,0:T(8,128)(2,1)S(1)}, bf16[16,7,128,128]{3,2,1,0:T(8,128)(2,1)}, u32[]{:S(2)}) %copy-start) | copy-done | bytes 3670040
  19.2 0.0 copy-start.1
  19.2 1.0 %copy-done.1 = bf16[16,128,128]{2,1,0:T(8,128)(2,1)S(1)} copy-done((bf16[16,128,128]{2,1,0:T(8,128)(2,1)S(1)}, bf16[16,128,128]{2,1,0:T(8,128)(2,1)}, u32[]{:S(2)}) %copy-start.1) | copy-done | bytes 524312
  20.2 0.0 copy-start.3
  20.2 0.7 %copy-done.3 = s32[16]{0:T(128)S(1)} copy-done((s32[16]{0:T(128)S(1)}, s32[16]{0:T(128)}, u32[]{:S(2)}) %copy-start.3) | copy-done | bytes 88
  20.9 0.0 copy-start.4
  20.9 0.7 %copy-done.4 = s32[16]{0:T(128)S(1)} copy-done((s32[16]{0:T(128)S(1)}, s32[16]{0:T(128)}, u32[]{:S(2)}) %copy-start.4) | copy-done | bytes 88
  21.6 2.1 %shard_map.66 = (bf16[912,128]{1,0:T(8,128)(2,1)S(1)}, bf16[912,128]{1,0:T(8,128)(2,1)S(1)}) custom-call(s32[16,7]{1,0:T(8,128)S(1)} %copy.12.cols, s32[16,7]{1,0:T(8,128)S(1)} %copy.8.target, s32[16]{0:T(128)S(1)} %copy-done.3, s32[16]{0:T(128)S(1)} %copy-done.4, bf16[16,7,128,128]{3,2,1,0:T(8,128)(2,1)S(1)} %copy-done, bf16[16,128,128]{2,1,0:T(8,128)(2,1)S(1)} %copy-done.1), custom_call_target="tpu_custom_call" | custom-call | flops 58720256 | bytes 917504 | tf_op jit(solution)/shard_map/pallas_call | solution.py:206
  23.7 1.9 %collective-permute-start.2 = (bf16[912,128]{1,0:T(8,128)(2,1)S(1)}, bf16[912,128]{1,0:T(8,128)(2,1)S(1)}, u32[]{:S(2)}, u32[]{:S(2)}) collective-permute-start(bf16[912,128]{1,0:T(8,128)(2,1)S(1)} %get-tuple-element.15), channel_id=1, source_target_pairs={{1,2},{3,4},{5,6},{7,8},{9,10},{11,12},{13,14},{15,16},{17,18},{19... | collective-permute-start | bytes 700424 | tf_op jit(solution)/shard_map/ppermute | solution.py:245
  25.6 4.0 %collective-permute-start.3 = (bf16[912,128]{1,0:T(8,128)(2,1)S(1)}, bf16[912,128]{1,0:T(8,128)(2,1)S(1)}, u32[]{:S(2)}, u32[]{:S(2)}) collective-permute-start(bf16[912,128]{1,0:T(8,128)(2,1)S(1)} %get-tuple-element.16), channel_id=1, source_target_pairs={{0,1},{2,3},{4,5},{6,7},{8,9},{10,11},{12,13},{14,15},{16,17},{18,... | collective-permute-start | bytes 700424 | tf_op jit(solution)/shard_map/ppermute | solution.py:246
  29.6 3.3 %collective-permute-start.4 = (bf16[2,128,128]{2,1,0:T(8,128)(2,1)S(1)}, bf16[2,128,128]{2,1,0:T(8,128)(2,1)S(1)}, u32[]{:S(2)}, u32[]{:S(2)}) collective-permute-start(bf16[2,128,128]{2,1,0:T(8,128)(2,1)S(1)} %get-tuple-element.18), channel_id=1, source_target_pairs={{0,2},{1,3},{2,4},{3,5},{4,6},{5,7},{6,8},{7,9},{8,10},{9,11},{10,... | collective-permute-start | bytes 196616 | tf_op jit(solution)/shard_map/ppermute | solution.py:247
  32.9 0.0 collective-permute-done.from_a
  32.9 7.4 %collective-permute-start.5 = (bf16[2,128,128]{2,1,0:T(8,128)(2,1)S(1)}, bf16[2,128,128]{2,1,0:T(8,128)(2,1)S(1)}, u32[]{:S(2)}, u32[]{:S(2)}) collective-permute-start(bf16[2,128,128]{2,1,0:T(8,128)(2,1)S(1)} %get-tuple-element.17), channel_id=1, source_target_pairs={{2,0},{3,1},{4,2},{5,3},{6,4},{7,5},{8,6},{9,7},{10,8},{11,9},{12,... | collective-permute-start | bytes 196616 | tf_op jit(solution)/shard_map/ppermute | solution.py:248
  40.4 8.8 %shard_map.64 = (f32[29,128,128]{2,1,0:T(8,128)S(1)}, bf16[72,128,128]{2,1,0:T(8,128)(2,1)S(1)}, s32[128]{0:T(128)S(1)}, s32[1]{0:T(128)}) custom-call(s32[16,7]{1,0:T(8,128)S(1)} %copy.12.cols, s32[16,7]{1,0:T(8,128)S(1)} %copy.8.target, s32[16]{0:T(128)S(1)} %copy-done.3, s32[16]{0:T(128)S(1)} %copy-done.4, bf16[16,7,128,128]{3,2,1,0:T(8,128)(2,1)S(1)} %copy-done, ...), custom_call_target="tpu_custom_call" | custom-call | flops 536870912 | bytes 8388608 | tf_op jit(solution)/shard_map/pallas_call | solution.py:206
  49.2 0.0 collective-permute-done.1.from_b
  49.2 0.0 copy-start.2
  49.2 2.6 %shard_map.65.acc = f32[29,128,128]{2,1,0:T(8,128)S(1)} custom-call(s32[16,7]{1,0:T(8,128)S(1)} %copy.12.cols, s32[128]{0:T(128)S(1)} %get-tuple-element.11.halo, s32[1]{0:T(128)} %get-tuple-element.12.halo_count, f32[29,128,128]{2,1,0:T(8,128)S(1)} %get-tuple-element.13.acc_in, bf16[72,128,128]{2,1,0:T(8,128)(2,1)S(1)} %get-tuple-element.14.left_halo, ...), custom_call_target="tpu_custom_call" | custom-call | flops 134217728 | bytes 6291456 | tf_op jit(solution)/shard_map/pallas_call | solution.py:206
  51.8 0.0 collective-permute-done.4.before
  51.8 0.0 collective-permute-done.5.after
  51.8 0.0 collective-permute-done.2.msg_a
  51.8 0.0 collective-permute-done.3.msg_b
  51.8 0.0 copy-done.2
  51.8 2.5 %shard_map.67 = bf16[4,7,128,128]{3,2,1,0:T(8,128)(2,1)} custom-call(s32[16,7]{1,0:T(8,128)S(1)} %copy.12.cols, f32[29,128,128]{2,1,0:T(8,128)S(1)} %shard_map.65.acc, bf16[912,128]{1,0:T(8,128)(2,1)S(1)} %collective-permute-done.2.msg_a, bf16[912,128]{1,0:T(8,128)(2,1)S(1)} %collective-permute-done.3.msg_b, bf16[16,128,128]{2,1,0:T(8,128)(2,1)S(1)} %copy-done.2, ...), custom_call_target="tpu_custom_call" | custom-call | flops 58720256 | bytes 5242880 | tf_op jit(solution)/shard_map/pallas_call | solution.py:206
  (1 shorter events, 0.0 us)
Async XLA Ops:
  0.0 32.9 %collective-permute-start = (bf16[16,128,128]{2,1,0:T(8,128)(2,1)}, bf16[16,128,128]{2,1,0:T(8,128)(2,1)S(1)}, u32[]{:S(2)}, u32[]{:S(2)}) collective-permute-start(bf16[16,128,128]{2,1,0:T(8,128)(2,1)} %p.5), channel_id=1, source_target_pairs={{1,2},{3,4},{5,6},{7,8},{9,10},{11,12},{13,14},{15,16},{17,18},{19... | collective-permute-start | bytes 1572872 | tf_op jit(solution)/shard_map/ppermute | solution.py:229
  3.5 45.7 %collective-permute-start.1 = (bf16[16,128,128]{2,1,0:T(8,128)(2,1)}, bf16[16,128,128]{2,1,0:T(8,128)(2,1)S(1)}, u32[]{:S(2)}, u32[]{:S(2)}) collective-permute-start(bf16[16,128,128]{2,1,0:T(8,128)(2,1)} %p.5), channel_id=1, source_target_pairs={{0,1},{2,3},{4,5},{6,7},{8,9},{10,11},{12,13},{14,15},{16,17},{18,... | collective-permute-start | bytes 1572872 | tf_op jit(solution)/shard_map/ppermute | solution.py:230
  17.2 2.0 %copy-start = (bf16[16,7,128,128]{3,2,1,0:T(8,128)(2,1)S(1)}, bf16[16,7,128,128]{3,2,1,0:T(8,128)(2,1)}, u32[]{:S(2)}) copy-start(bf16[16,7,128,128]{3,2,1,0:T(8,128)(2,1)} %a.3) | copy-start | bytes 11010052
  19.2 1.0 %copy-start.1 = (bf16[16,128,128]{2,1,0:T(8,128)(2,1)S(1)}, bf16[16,128,128]{2,1,0:T(8,128)(2,1)}, u32[]{:S(2)}) copy-start(bf16[16,128,128]{2,1,0:T(8,128)(2,1)} %p.5) | copy-start | bytes 1572868
  20.2 0.7 %copy-start.3 = (s32[16]{0:T(128)S(1)}, s32[16]{0:T(128)}, u32[]{:S(2)}) copy-start(s32[16]{0:T(128)} %agg.3) | copy-start | bytes 196
  20.9 0.7 %copy-start.4 = (s32[16]{0:T(128)S(1)}, s32[16]{0:T(128)}, u32[]{:S(2)}) copy-start(s32[16]{0:T(128)} %refine.3) | copy-start | bytes 196
  23.7 28.1 %collective-permute-start.2 = (bf16[912,128]{1,0:T(8,128)(2,1)S(1)}, bf16[912,128]{1,0:T(8,128)(2,1)S(1)}, u32[]{:S(2)}, u32[]{:S(2)}) collective-permute-start(bf16[912,128]{1,0:T(8,128)(2,1)S(1)} %get-tuple-element.15), channel_id=1, source_target_pairs={{1,2},{3,4},{5,6},{7,8},{9,10},{11,12},{13,14},{15,16},{17,18},{19... | collective-permute-start | bytes 700424 | tf_op jit(solution)/shard_map/ppermute | solution.py:245
  25.6 26.2 %collective-permute-start.3 = (bf16[912,128]{1,0:T(8,128)(2,1)S(1)}, bf16[912,128]{1,0:T(8,128)(2,1)S(1)}, u32[]{:S(2)}, u32[]{:S(2)}) collective-permute-start(bf16[912,128]{1,0:T(8,128)(2,1)S(1)} %get-tuple-element.16), channel_id=1, source_target_pairs={{0,1},{2,3},{4,5},{6,7},{8,9},{10,11},{12,13},{14,15},{16,17},{18,... | collective-permute-start | bytes 700424 | tf_op jit(solution)/shard_map/ppermute | solution.py:246
  29.6 22.1 %collective-permute-start.4 = (bf16[2,128,128]{2,1,0:T(8,128)(2,1)S(1)}, bf16[2,128,128]{2,1,0:T(8,128)(2,1)S(1)}, u32[]{:S(2)}, u32[]{:S(2)}) collective-permute-start(bf16[2,128,128]{2,1,0:T(8,128)(2,1)S(1)} %get-tuple-element.18), channel_id=1, source_target_pairs={{0,2},{1,3},{2,4},{3,5},{4,6},{5,7},{6,8},{7,9},{8,10},{9,11},{10,... | collective-permute-start | bytes 196616 | tf_op jit(solution)/shard_map/ppermute | solution.py:247
  32.9 18.9 %collective-permute-start.5 = (bf16[2,128,128]{2,1,0:T(8,128)(2,1)S(1)}, bf16[2,128,128]{2,1,0:T(8,128)(2,1)S(1)}, u32[]{:S(2)}, u32[]{:S(2)}) collective-permute-start(bf16[2,128,128]{2,1,0:T(8,128)(2,1)S(1)} %get-tuple-element.17), channel_id=1, source_target_pairs={{2,0},{3,1},{4,2},{5,3},{6,4},{7,5},{8,6},{9,7},{10,8},{11,9},{12,... | collective-permute-start | bytes 196616 | tf_op jit(solution)/shard_map/ppermute | solution.py:248
  49.2 2.6 %copy-start.2 = (bf16[16,128,128]{2,1,0:T(8,128)(2,1)S(1)}, bf16[16,128,128]{2,1,0:T(8,128)(2,1)}, u32[]{:S(2)}) copy-start(bf16[16,128,128]{2,1,0:T(8,128)(2,1)} %p.5) | copy-start | bytes 1572868

commit v2 on v0

v2 whole, which is shorter than its diff:
```python
import jax
import jax.numpy as jnp
from jax import lax
from jax.experimental import pallas as pl
from jax.experimental.pallas import tpu as pltpu
from jax.sharding import PartitionSpec as P

ROWS = 16
DIM = 128
SLOTS = 7
LIVE = 3
COARSE = 4
SEGS = COARSE * SLOTS
UNROLL = 8
HALO_MAX = 64 + UNROLL
EDGE_MAX = 16 + UNROLL
LIST = 128
AXES = ("dom", "sub")
F32 = jnp.float32
BF16 = jnp.bfloat16

SMEM = pl.BlockSpec(memory_space=pltpu.SMEM)
VMEM = pl.BlockSpec(memory_space=pltpu.VMEM)
SHAPE = jax.ShapeDtypeStruct
BLOCK_COST = 2 * DIM**3


def dot(x, y):
    return jnp.dot(x, y, preferred_element_type=F32)


def add_items(count, codes, left, right, acc, by_slot):
    def step(at, carry):
        parts = []
        for j in range(UNROLL):
            n = at * UNROLL + j
            code = codes[n]
            slot = (code & 127) if by_slot else n
            parts.append((code >> 12, dot(left[slot], right((code >> 7) & 31))))
        for seg, part in parts:
            acc[seg] += part
        return carry

    lax.fori_loop(0, (count + UNROLL - 1) // UNROLL, step, 0)


def list_kernel(ints, own, halo, edge, counts):
    first_row = ints[0, 0]
    first_coarse = first_row // COARSE

    def listing(row, found):
        own_n, halo_n, edge_n = found
        group = ints[2 * SLOTS, row] - first_coarse
        inside = (group >= 0) & (group < COARSE)
        fine = ints[2 * SLOTS + 1, row] == 1
        for k in range(SLOTS):
            live = True if k < LIVE else fine
            column = ints[k, row] - first_row
            aim = ints[SLOTS + k, row]
            here = (column >= 0) & (column < ROWS)
            place = (jnp.where(column < 0, column + ROWS, column) & 31) * 128
            side = jnp.where(group < 0, 0, SLOTS) + aim
            home = group * SLOTS + aim
            slot = row * SLOTS + k
            own[own_n] = slot + place + jnp.where(inside, home, SEGS + 1 + side) * 4096
            halo[halo_n] = slot + place + home * 4096
            edge[edge_n] = slot + place + side * 4096
            away = live & jnp.logical_not(here)
            own_n += (live & here).astype(jnp.int32)
            halo_n += (away & inside).astype(jnp.int32)
            edge_n += (away & jnp.logical_not(inside)).astype(jnp.int32)
        return own_n, halo_n, edge_n

    own_n, halo_n, edge_n = lax.fori_loop(0, ROWS, listing, (0, 0, 0))
    for j in range(UNROLL):
        own[own_n + j] = SEGS * 4096
        halo[halo_n + j] = SEGS * 4096
        edge[edge_n + j] = 2 * SLOTS * 4096
    counts[0] = halo_n
    counts[1] = edge_n
    counts[2] = (first_row // ROWS) % 2
    counts[3] = own_n


def own_kernel(own, halo, edge, counts, a, p, acc, edge_acc, left_halo, left_edge, left, total):
    total[...] = jnp.zeros(total.shape, F32)
    for row in range(ROWS):
        turned = p[row].T
        for k in range(0, SLOTS, 2):
            if k + 1 < SLOTS:
                both = dot(turned, jnp.concatenate([a[row, k], a[row, k + 1]], axis=1)).astype(BF16)
                left[row * SLOTS + k] = both[:, :DIM]
                left[row * SLOTS + k + 1] = both[:, DIM:]
            else:
                left[row * SLOTS + k] = dot(turned, a[row, k]).astype(BF16)
    add_items(counts[3], own, left, lambda at: p[at & 15], total, True)
    acc[...] = total[: SEGS + 1]
    edge_acc[...] = total[SEGS + 1 :]

    def keep_in(codes, kept):
        def keep(at, carry):
            for j in range(UNROLL):
                n = at * UNROLL + j
                kept[n] = left[codes[n] & 127]
            return carry

        return keep

    lax.fori_loop(0, (counts[0] + UNROLL - 1) // UNROLL, keep_in(halo, left_halo), 0)
    lax.fori_loop(0, (counts[1] + UNROLL - 1) // UNROLL, keep_in(edge, left_edge), 0)


def picker(odd, from_a, from_b):
    return lambda at: jnp.where((at >> 4) == odd, from_a[at & 15], from_b[at & 15])


def edge_kernel(edge, counts, edge_acc, left_edge, from_a, from_b, msg_a, msg_b, total):
    odd = counts[2]
    total[...] = edge_acc[...]
    add_items(counts[1], edge, left_edge, picker(odd, from_a, from_b), total, False)
    for s in range(SLOTS):
        msg_a[s] = total[odd * SLOTS + s].astype(BF16)
        msg_b[s] = total[(1 - odd) * SLOTS + s].astype(BF16)


def halo_kernel(halo, counts, acc_in, left_halo, from_a, from_b, acc):
    acc[...] = acc_in[...]
    add_items(counts[0], halo, left_halo, picker(counts[2], from_a, from_b), acc, False)


def last_kernel(counts, acc, got_a, got_b, out):
    odd = counts[2] == 1
    for s in range(SEGS):
        value = acc[s]
        if s < SLOTS:
            value = value + jnp.where(odd, got_b[s], got_a[s]).astype(F32)
        if s >= SEGS - SLOTS:
            at = s - (SEGS - SLOTS)
            value = value + jnp.where(odd, got_a[at], got_b[at]).astype(F32)
        out[s // SLOTS, s % SLOTS] = value.astype(BF16)


def call(kernel, ins, smems, outs, out_specs, scratch, blocks, size):
    return pl.pallas_call(
        kernel,
        out_shape=outs,
        in_specs=[SMEM] * smems + [VMEM] * (len(ins) - smems),
        out_specs=out_specs,
        scratch_shapes=scratch,
        cost_estimate=pl.CostEstimate(flops=blocks * BLOCK_COST, bytes_accessed=size, transcendentals=0),
        compiler_params=pltpu.CompilerParams(vmem_limit_bytes=36 * 1024 * 1024),
    )(*ins)


def list_part(ints):
    return call(
        list_kernel,
        (ints,),
        1,
        [SHAPE((LIST,), jnp.int32)] * 3 + [SHAPE((4,), jnp.int32)],
        [SMEM] * 4,
        [],
        256,
        1 << 20,
    )


def own_part(own, halo, edge, counts, a_blocks, p_blocks):
    return call(
        own_kernel,
        (own, halo, edge, counts, a_blocks, p_blocks),
        4,
        [
            SHAPE((SEGS + 1, DIM, DIM), F32),
            SHAPE((2 * SLOTS + 1, DIM, DIM), F32),
            SHAPE((HALO_MAX, DIM, DIM), BF16),
            SHAPE((EDGE_MAX, DIM, DIM), BF16),
        ],
        [VMEM] * 4,
        [
            pltpu.VMEM((ROWS * SLOTS, DIM, DIM), BF16),
            pltpu.VMEM((SEGS + 2 * SLOTS + 2, DIM, DIM), F32),
        ],
        128,
        8 << 20,
    )


def edge_part(edge, counts, edge_acc, left_edge, from_a, from_b):
    return call(
        edge_kernel,
        (edge, counts, edge_acc, left_edge, from_a, from_b),
        2,
        [SHAPE((SLOTS, DIM, DIM), BF16)] * 2,
        [VMEM] * 2,
        [pltpu.VMEM((2 * SLOTS + 1, DIM, DIM), F32)],
        8,
        2 << 20,
    )


def halo_part(halo, counts, acc, left_halo, from_a, from_b):
    return call(
        halo_kernel,
        (halo, counts, acc, left_halo, from_a, from_b),
        2,
        SHAPE((SEGS + 1, DIM, DIM), F32),
        VMEM,
        [],
        32,
        6 << 20,
    )


def last_part(counts, acc, got_a, got_b):
    return call(
        last_kernel,
        (counts, acc, got_a, got_b),
        1,
        SHAPE((COARSE, SLOTS, DIM, DIM), BF16),
        VMEM,
        [],
        1,
        4 << 20,
    )


def body(a_blocks, p_blocks, a_cols, a_target, agg, refine):
    count = lax.axis_size(AXES)
    odd_pairs = [(i, i + 1) for i in range(1, count - 1, 2)]
    even_pairs = [(i, i + 1) for i in range(0, count, 2)]
    pairs_a = odd_pairs + [(j, i) for i, j in odd_pairs]
    pairs_b = even_pairs + [(j, i) for i, j in even_pairs]
    ints = jnp.concatenate([a_cols.T, a_target.T, agg[None], refine[None]])

    from_a = lax.ppermute(p_blocks, AXES, pairs_a)
    from_b = lax.ppermute(p_blocks, AXES, pairs_b)
    own, halo, edge, counts = list_part(ints)
    acc, edge_acc, left_halo, left_edge = own_part(own, halo, edge, counts, a_blocks, p_blocks)
    msg_a, msg_b = edge_part(edge, counts, edge_acc, left_edge, from_a, from_b)
    got_a = lax.ppermute(msg_a, AXES, pairs_a)
    got_b = lax.ppermute(msg_b, AXES, pairs_b)
    acc = halo_part(halo, counts, acc, left_halo, from_a, from_b)
    return last_part(counts, acc, got_a, got_b)


def solution(mesh):
    return jax.shard_map(
        body,
        mesh=mesh,
        in_specs=(
            P(AXES, None, None, None),
            P(AXES, None, None),
            P(AXES, None),
            P(AXES, None),
            P(AXES),
            P(AXES),
        ),
        out_specs=P(AXES, None, None, None),
        check_vma=False,
    )
```

time: 131 us -> 42 us (0.32)
  waiting for transfers between devices: 44.3 us -> 6.11 us
  other arithmetic: 37.2 us -> 0.75 us
  local copies, waits for them, and re-layouts: 14.6 us -> 1.04 us
  matrix products: 12.4 us -> 0 us
  Pallas kernels: 0 us -> 10.5 us
  starting transfers between devices: 21.3 us -> 23.3 us
    ppermute x4, waiting for transfers between devices: 44.3 us -> 6.11 us  [the longest x1 2.95 us: body(): got_a = lax.ppermute(msg_a, AXES, pairs_a)]
    scatter-add x1 -> x0, other arithmetic: 22.6 us -> none  [body(): jax.ops.segment_sum(contrib, segment, num_segments=3 * own_total + 1)[:-1]]
    dot_general x1 -> x0, matrix products: 12.4 us -> none  [body(): jnp.einsum('nfb,nfc->nbc', p_blocks[row_of], products, preferred_element_...]
    pallas_call x0 -> x5, Pallas kernels: none -> 10.5 us  [call(): pl.pallas_call(kernel, out_shape=outs, in_specs=[SMEM] * smems + [VMEM] *...]
    select_n x3 -> x0, other arithmetic: 10 us -> none  [the longest x1 10 us: body(): jnp.where(inside, (item_coarse + coarse_count) * coarse_slots + target_of...]
    gather x3 -> x0, local copies, waits for them, and re-layouts: 7.78 us -> none  [the longest x1 4.09 us: body(): p_blocks[row_of]]
    broadcast_in_dim x2 -> x0, local copies, waits for them, and re-layouts: 3.09 us -> none  [the longest x1 3.08 us: body(): jax.ops.segment_sum(contrib, segment, num_segments=3 * own_total + 1)[:-1]]
    convert_element_type x1 -> x0, other arithmetic: 2.96 us -> none  [body(): result.reshape(coarse_count, coarse_slots, block_dim, block_dim)]
  transfers between devices with their start and end apart: 4 -> 4, of which waited for: 2 -> 3; matrix products, arithmetic and copies ran while one was open for 13% -> 2% of each run, Pallas kernels for 0% -> 19%
where the time goes in v2:
time: 42 us; the launch traced here: 41.8 us
  starting transfers between devices  23.3 us (55%)
  Pallas kernels  10.5 us (25%)
  waiting for transfers between devices  6.11 us (15%)
  local copies, waits for them, and re-layouts  1.04 us (2%)
  other arithmetic  0.75 us (2%)
    ppermute x1, starting transfers between devices, body(): from_a = lax.ppermute(p_blocks, AXES, pairs_a)  13.8 us
    pallas_call x5, Pallas kernels, call(): pl.pallas_call(kernel, out_shape=outs, in_specs=[SMEM] * smems + [VMEM] *...  10.5 us
    ppermute x1, starting transfers between devices, body(): got_a = lax.ppermute(msg_a, AXES, pairs_a)  5.65 us
    ppermute x1, waiting for transfers between devices, body(): got_a = lax.ppermute(msg_a, AXES, pairs_a)  2.95 us
    ppermute x1, starting transfers between devices, body(): from_b = lax.ppermute(p_blocks, AXES, pairs_b)  1.92 us
    ppermute x1, starting transfers between devices, body(): got_b = lax.ppermute(msg_b, AXES, pairs_b)  1.92 us
    ppermute x1, waiting for transfers between devices, body(): from_a = lax.ppermute(p_blocks, AXES, pairs_a)  1.78 us
    ppermute x1, waiting for transfers between devices, body(): got_b = lax.ppermute(msg_b, AXES, pairs_b)  1.38 us
  transfers between devices with their start and end apart: 4, of which 3 were waited for; matrix products, arithmetic and copies ran while one was open for 2% of the time, Pallas kernels for 19%

profile of v2, /device:TPU:6, one launch (start us, length us, event | category | flops | bytes accessed | tf_op | source)
XLA Modules:
  0.0 41.8 jit_solution(3264459324584740051)
XLA Ops:
  0.0 0.0 copy-start
  0.0 13.8 %collective-permute-start = (bf16[16,128,128]{2,1,0:T(8,128)(2,1)}, bf16[16,128,128]{2,1,0:T(8,128)(2,1)S(1)}, u32[]{:S(2)}, u32[]{:S(2)}) collective-permute-start(bf16[16,128,128]{2,1,0:T(8,128)(2,1)} %p.1), channel_id=1, source_target_pairs={{1,2},{3,4},{5,6},{7,8},{9,10},{11,12},{13,14},{15,16},{17,18},{19... | collective-permute-start | bytes 1572872 | tf_op jit(solution)/shard_map/ppermute | solution.py:236
  13.8 1.9 %collective-permute-start.1 = (bf16[16,128,128]{2,1,0:T(8,128)(2,1)}, bf16[16,128,128]{2,1,0:T(8,128)(2,1)S(1)}, u32[]{:S(2)}, u32[]{:S(2)}) collective-permute-start(bf16[16,128,128]{2,1,0:T(8,128)(2,1)} %p.1), channel_id=1, source_target_pairs={{0,1},{2,3},{4,5},{6,7},{8,9},{10,11},{12,13},{14,15},{16,17},{18,... | collective-permute-start | bytes 1572872 | tf_op jit(solution)/shard_map/ppermute | solution.py:237
  15.8 0.7 %pad_add_fusion.ints = s32[16,16]{1,0:T(8,128)S(1)} fusion(s32[1,16]{1,0:T(1,128)} %bitcast.6, s32[1,16]{1,0:T(1,128)} %bitcast.7, s32[7,16]{1,0:T(8,128)} %bitcast.4, s32[7,16]{1,0:T(8,128)} %bitcast.5), kind=kLoop, calls=%fused_computation | loop fusion | flops 768 | bytes 2048 | tf_op jit(solution)/shard_map/concatenate | solution.py:234
  16.5 2.8 %shard_map.64 = (s32[128]{0:T(128)S(1)}, s32[128]{0:T(128)S(1)}, s32[128]{0:T(128)S(1)}, s32[4]{0:T(128)S(1)}) custom-call(s32[16,16]{1,0:T(8,128)S(1)} %pad_add_fusion.ints), custom_call_target="tpu_custom_call" | custom-call | flops 1073741824 | bytes 1048576 | tf_op jit(solution)/shard_map/pallas_call | solution.py:144
  19.3 0.0 copy-done
  19.3 0.0 copy-start.1
  19.3 1.0 %copy-done.1 = bf16[16,128,128]{2,1,0:T(8,128)(2,1)S(1)} copy-done((bf16[16,128,128]{2,1,0:T(8,128)(2,1)S(1)}, bf16[16,128,128]{2,1,0:T(8,128)(2,1)}, u32[]{:S(2)}) %copy-start.1) | copy-done | bytes 524312
  20.4 3.5 %shard_map.65 = (f32[29,128,128]{2,1,0:T(8,128)S(1)}, f32[15,128,128]{2,1,0:T(8,128)S(1)}, bf16[72,128,128]{2,1,0:T(8,128)(2,1)S(1)}, bf16[24,128,128]{2,1,0:T(8,128)(2,1)S(1)}) custom-call(s32[128]{0:T(128)S(1)} %get-tuple-element.17.own, s32[128]{0:T(128)S(1)} %get-tuple-element.16.halo, s32[128]{0:T(128)S(1)} %get-tuple-element.18.edge, ...), custom_call_target="tpu_custom_call" | custom-call | flops 536870912 | bytes 8388608 | tf_op jit(solution)/shard_map/pallas_call | solution.py:144
  23.9 1.8 %collective-permute-done.from_a = bf16[16,128,128]{2,1,0:T(8,128)(2,1)S(1)} collective-permute-done((bf16[16,128,128]{2,1,0:T(8,128)(2,1)}, bf16[16,128,128]{2,1,0:T(8,128)(2,1)S(1)}, u32[]{:S(2)}, u32[]{:S(2)}) %collective-permute-start) | collective-permute-done | bytes 524320 | tf_op jit(solution)/shard_map/ppermute | solution.py:236
  25.7 0.0 collective-permute-done.1.from_b
  25.7 0.9 %shard_map.67 = (bf16[7,128,128]{2,1,0:T(8,128)(2,1)S(1)}, bf16[7,128,128]{2,1,0:T(8,128)(2,1)S(1)}) custom-call(s32[128]{0:T(128)S(1)} %get-tuple-element.18.edge, s32[4]{0:T(128)S(1)} %get-tuple-element.15.counts, f32[15,128,128]{2,1,0:T(8,128)S(1)} %get-tuple-element.21.edge_acc, bf16[24,128,128]{2,1,0:T(8,128)(2,1)S(1)} %get-tuple-element.22.left_edge, ...), custom_call_target="tpu_custom_call" | custom-call | flops 33554432 | bytes 2097152 | tf_op jit(solution)/shard_map/pallas_call | solution.py:144
  26.6 5.6 %collective-permute-start.2 = (bf16[7,128,128]{2,1,0:T(8,128)(2,1)S(1)}, bf16[7,128,128]{2,1,0:T(8,128)(2,1)S(1)}, u32[]{:S(2)}, u32[]{:S(2)}) collective-permute-start(bf16[7,128,128]{2,1,0:T(8,128)(2,1)S(1)} %get-tuple-element.23), channel_id=1, source_target_pairs={{1,2},{3,4},{5,6},{7,8},{9,10},{11,12},{13,14},{15,16},{17,18},{19... | collective-permute-start | bytes 688136 | tf_op jit(solution)/shard_map/ppermute | solution.py:241
  32.2 1.9 %collective-permute-start.3 = (bf16[7,128,128]{2,1,0:T(8,128)(2,1)S(1)}, bf16[7,128,128]{2,1,0:T(8,128)(2,1)S(1)}, u32[]{:S(2)}, u32[]{:S(2)}) collective-permute-start(bf16[7,128,128]{2,1,0:T(8,128)(2,1)S(1)} %get-tuple-element.24), channel_id=1, source_target_pairs={{0,1},{2,3},{4,5},{6,7},{8,9},{10,11},{12,13},{14,15},{16,17},{18,... | collective-permute-start | bytes 688136 | tf_op jit(solution)/shard_map/ppermute | solution.py:242
  34.2 1.7 %shard_map.66.acc = f32[29,128,128]{2,1,0:T(8,128)S(1)} custom-call(s32[128]{0:T(128)S(1)} %get-tuple-element.16.halo, s32[4]{0:T(128)S(1)} %get-tuple-element.15.counts, f32[29,128,128]{2,1,0:T(8,128)S(1)} %get-tuple-element.19.acc_in, bf16[72,128,128]{2,1,0:T(8,128)(2,1)S(1)} %get-tuple-element.20.left_halo, ...), custom_call_target="tpu_custom_call" | custom-call | flops 134217728 | bytes 6291456 | tf_op jit(solution)/shard_map/pallas_call | solution.py:144
  35.8 3.0 %collective-permute-done.2.got_a = bf16[7,128,128]{2,1,0:T(8,128)(2,1)S(1)} collective-permute-done((bf16[7,128,128]{2,1,0:T(8,128)(2,1)S(1)}, bf16[7,128,128]{2,1,0:T(8,128)(2,1)S(1)}, u32[]{:S(2)}, u32[]{:S(2)}) %collective-permute-start.2) | collective-permute-done | bytes 229408 | tf_op jit(solution)/shard_map/ppermute | solution.py:241
  38.8 1.4 %collective-permute-done.3.got_b = bf16[7,128,128]{2,1,0:T(8,128)(2,1)S(1)} collective-permute-done((bf16[7,128,128]{2,1,0:T(8,128)(2,1)S(1)}, bf16[7,128,128]{2,1,0:T(8,128)(2,1)S(1)}, u32[]{:S(2)}, u32[]{:S(2)}) %collective-permute-start.3) | collective-permute-done | bytes 229408 | tf_op jit(solution)/shard_map/ppermute | solution.py:242
  40.1 1.6 %shard_map.68 = bf16[4,7,128,128]{3,2,1,0:T(8,128)(2,1)} custom-call(s32[4]{0:T(128)S(1)} %get-tuple-element.15.counts, f32[29,128,128]{2,1,0:T(8,128)S(1)} %shard_map.66.acc, bf16[7,128,128]{2,1,0:T(8,128)(2,1)S(1)} %collective-permute-done.2.got_a, bf16[7,128,128]{2,1,0:T(8,128)(2,1)S(1)} %collective-permute-done.3.got_b), custom_call_target="tpu_custom_call" | custom-call | flops 4194304 | bytes 4194304 | tf_op jit(solution)/shard_map/pallas_call | solution.py:144
Async XLA Ops:
  0.0 19.3 %copy-start = (bf16[16,7,128,128]{3,2,1,0:T(8,128)(2,1)S(1)}, bf16[16,7,128,128]{3,2,1,0:T(8,128)(2,1)}, u32[]{:S(2)}) copy-start(bf16[16,7,128,128]{3,2,1,0:T(8,128)(2,1)} %a.1) | copy-start | bytes 11010052
  0.0 25.7 %collective-permute-start = (bf16[16,128,128]{2,1,0:T(8,128)(2,1)}, bf16[16,128,128]{2,1,0:T(8,128)(2,1)S(1)}, u32[]{:S(2)}, u32[]{:S(2)}) collective-permute-start(bf16[16,128,128]{2,1,0:T(8,128)(2,1)} %p.1), channel_id=1, source_target_pairs={{1,2},{3,4},{5,6},{7,8},{9,10},{11,12},{13,14},{15,16},{17,18},{19... | collective-permute-start | bytes 1572872 | tf_op jit(solution)/shard_map/ppermute | solution.py:236
  13.8 11.8 %collective-permute-start.1 = (bf16[16,128,128]{2,1,0:T(8,128)(2,1)}, bf16[16,128,128]{2,1,0:T(8,128)(2,1)S(1)}, u32[]{:S(2)}, u32[]{:S(2)}) collective-permute-start(bf16[16,128,128]{2,1,0:T(8,128)(2,1)} %p.1), channel_id=1, source_target_pairs={{0,1},{2,3},{4,5},{6,7},{8,9},{10,11},{12,13},{14,15},{16,17},{18,... | collective-permute-start | bytes 1572872 | tf_op jit(solution)/shard_map/ppermute | solution.py:237
  19.3 1.0 %copy-start.1 = (bf16[16,128,128]{2,1,0:T(8,128)(2,1)S(1)}, bf16[16,128,128]{2,1,0:T(8,128)(2,1)}, u32[]{:S(2)}) copy-start(bf16[16,128,128]{2,1,0:T(8,128)(2,1)} %p.1) | copy-start | bytes 1572868
  26.6 12.2 %collective-permute-start.2 = (bf16[7,128,128]{2,1,0:T(8,128)(2,1)S(1)}, bf16[7,128,128]{2,1,0:T(8,128)(2,1)S(1)}, u32[]{:S(2)}, u32[]{:S(2)}) collective-permute-start(bf16[7,128,128]{2,1,0:T(8,128)(2,1)S(1)} %get-tuple-element.23), channel_id=1, source_target_pairs={{1,2},{3,4},{5,6},{7,8},{9,10},{11,12},{13,14},{15,16},{17,18},{19... | collective-permute-start | bytes 688136 | tf_op jit(solution)/shard_map/ppermute | solution.py:241
  32.2 7.9 %collective-permute-start.3 = (bf16[7,128,128]{2,1,0:T(8,128)(2,1)S(1)}, bf16[7,128,128]{2,1,0:T(8,128)(2,1)S(1)}, u32[]{:S(2)}, u32[]{:S(2)}) collective-permute-start(bf16[7,128,128]{2,1,0:T(8,128)(2,1)S(1)} %get-tuple-element.24), channel_id=1, source_target_pairs={{0,1},{2,3},{4,5},{6,7},{8,9},{10,11},{12,13},{14,15},{16,17},{18,... | collective-permute-start | bytes 688136 | tf_op jit(solution)/shard_map/ppermute | solution.py:242

commit v3 on v2

v3 whole, which is shorter than its diff:
```python
import jax
import jax.numpy as jnp
from jax import lax
from jax.experimental import pallas as pl
from jax.experimental.pallas import tpu as pltpu
from jax.sharding import PartitionSpec as P

ROWS = 16
DIM = 128
SLOTS = 7
LIVE = 3
COARSE = 4
SEGS = COARSE * SLOTS
UNROLL = 8
HALO_MAX = 64 + UNROLL
EDGE_MAX = 16 + UNROLL
LIST = 128
OWN, HALO, EDGE, COUNTS = 0, LIST, 2 * LIST, 3 * LIST
AXES = ("dom", "sub")
F32 = jnp.float32
BF16 = jnp.bfloat16

SMEM = pl.BlockSpec(memory_space=pltpu.SMEM)
VMEM = pl.BlockSpec(memory_space=pltpu.VMEM)
ANY = pl.BlockSpec(memory_space=pl.ANY)
SHAPE = jax.ShapeDtypeStruct
BLOCK_COST = 2 * DIM**3


def color_of(edge):
    return 2 if edge % 128 == 126 else edge % 2


def color_in_kernel(edge):
    return jnp.where((edge & 127) == 126, 2, edge & 1)


def dot(x, y):
    return jnp.dot(x, y, preferred_element_type=F32)


def add_items(count, table, base, left, right, acc, by_slot):
    def step(at, carry):
        parts = []
        for j in range(UNROLL):
            n = at * UNROLL + j
            code = table[base + n]
            slot = (code & 127) if by_slot else n
            parts.append((code >> 12, dot(left[slot], right((code >> 7) & 31))))
        for seg, part in parts:
            acc[seg] += part
        return carry

    lax.fori_loop(0, (count + UNROLL - 1) // UNROLL, step, 0)


def list_kernel(ints, table):
    first_row = ints[0, 0]
    first_coarse = first_row // COARSE

    def listing(row, found):
        own_n, halo_n, edge_n = found
        group = ints[2 * SLOTS, row] - first_coarse
        inside = (group >= 0) & (group < COARSE)
        fine = ints[2 * SLOTS + 1, row] == 1
        for k in range(SLOTS):
            live = True if k < LIVE else fine
            column = ints[k, row] - first_row
            aim = ints[SLOTS + k, row]
            here = (column >= 0) & (column < ROWS)
            place = (jnp.where(column < 0, column + ROWS, column) & 31) * 128
            side = jnp.where(group < 0, 0, SLOTS) + aim
            home = group * SLOTS + aim
            slot = row * SLOTS + k
            table[OWN + own_n] = slot + place + jnp.where(inside, home, SEGS + 1 + side) * 4096
            table[HALO + halo_n] = slot + place + home * 4096
            table[EDGE + edge_n] = slot + place + side * 4096
            away = live & jnp.logical_not(here)
            own_n += (live & here).astype(jnp.int32)
            halo_n += (away & inside).astype(jnp.int32)
            edge_n += (away & jnp.logical_not(inside)).astype(jnp.int32)
        return own_n, halo_n, edge_n

    own_n, halo_n, edge_n = lax.fori_loop(0, ROWS, listing, (0, 0, 0))
    for j in range(UNROLL):
        table[OWN + own_n + j] = SEGS * 4096
        table[HALO + halo_n + j] = SEGS * 4096
        table[EDGE + edge_n + j] = 2 * SLOTS * 4096
    table[COUNTS + 0] = halo_n
    table[COUNTS + 1] = edge_n
    table[COUNTS + 2] = own_n
    table[COUNTS + 3] = color_in_kernel(first_row // ROWS - 1)
    table[COUNTS + 4] = color_in_kernel(first_row // ROWS)


def own_kernel(table, a, p, acc, edge_acc, left_halo, left_edge, left, total):
    total[...] = jnp.zeros(total.shape, F32)
    for row in range(ROWS):
        turned = p[row].T
        for k in range(0, SLOTS, 2):
            if k + 1 < SLOTS:
                both = dot(turned, jnp.concatenate([a[row, k], a[row, k + 1]], axis=1)).astype(BF16)
                left[row * SLOTS + k] = both[:, :DIM]
                left[row * SLOTS + k + 1] = both[:, DIM:]
            else:
                left[row * SLOTS + k] = dot(turned, a[row, k]).astype(BF16)
    add_items(table[COUNTS + 2], table, OWN, left, lambda at: p[at & 15], total, True)
    acc[...] = total[: SEGS + 1]
    edge_acc[...] = total[SEGS + 1 :]

    def keep_in(base, kept):
        def keep(at, carry):
            for j in range(UNROLL):
                n = at * UNROLL + j
                kept[n] = left[table[base + n] & 127]
            return carry

        return keep

    lax.fori_loop(0, (table[COUNTS + 0] + UNROLL - 1) // UNROLL, keep_in(HALO, left_halo), 0)
    lax.fori_loop(0, (table[COUNTS + 1] + UNROLL - 1) // UNROLL, keep_in(EDGE, left_edge), 0)


def choose(color, values):
    return jnp.where(color == 0, values[0], jnp.where(color == 1, values[1], values[2]))


def picker(table, sources):
    def right(at):
        color = jnp.where(at < ROWS, table[COUNTS + 3], table[COUNTS + 4])
        return choose(color, [source[at & 15] for source in sources])

    return right


def edge_kernel(table, edge_acc, left_edge, from_0, from_1, from_2, msg_0, msg_1, msg_2, total):
    total[...] = edge_acc[...]
    add_items(table[COUNTS + 1], table, EDGE, left_edge, picker(table, (from_0, from_1, from_2)), total, False)
    for color, msg in enumerate((msg_0, msg_1, msg_2)):
        side = jnp.where(table[COUNTS + 4] == color, SLOTS, 0)
        for s in range(SLOTS):
            msg[s] = total[side + s].astype(BF16)


def halo_kernel(table, acc_in, left_halo, from_0, from_1, from_2, acc, out, total, inner, sem):
    total[...] = acc_in[...]
    add_items(table[COUNTS + 0], table, HALO, left_halo, picker(table, (from_0, from_1, from_2)), total, False)
    for s in range(SLOTS, SEGS - SLOTS):
        inner[s // SLOTS - 1, s % SLOTS] = total[s].astype(BF16)
    copy = pltpu.make_async_copy(inner, out.at[pl.ds(1, COARSE - 2)], sem)
    copy.start()
    acc[:SLOTS] = total[:SLOTS]
    acc[SLOTS:] = total[SEGS - SLOTS : SEGS]
    copy.wait()


def last_kernel(acc, got_0, got_1, got_2, out_in, out, outer, sems):
    got = (got_0, got_1, got_2)
    device = lax.axis_index(AXES[0]) * lax.axis_size(AXES[1]) + lax.axis_index(AXES[1])
    copies = []
    for side, row in enumerate((0, COARSE - 1)):
        color = color_in_kernel(device - 1 + side)
        for s in range(SLOTS):
            value = acc[side * SLOTS + s] + choose(color, [g[s] for g in got]).astype(F32)
            outer[side, s] = value.astype(BF16)
        copies.append(pltpu.make_async_copy(outer.at[side], out.at[row], sems.at[side]))
        copies[-1].start()
    for copy in copies:
        copy.wait()


def call(kernel, ins, smems, outs, out_specs, scratch, blocks, size, anys=0, aliases={}):
    return pl.pallas_call(
        kernel,
        out_shape=outs,
        in_specs=[SMEM] * smems + [VMEM] * (len(ins) - smems - anys) + [ANY] * anys,
        out_specs=out_specs,
        scratch_shapes=scratch,
        input_output_aliases=aliases,
        cost_estimate=pl.CostEstimate(flops=blocks * BLOCK_COST, bytes_accessed=size, transcendentals=0),
        compiler_params=pltpu.CompilerParams(vmem_limit_bytes=36 * 1024 * 1024),
    )(*ins)


def list_part(ints):
    return call(
        list_kernel,
        (ints,),
        1,
        SHAPE((COUNTS + 16,), jnp.int32),
        SMEM,
        [],
        2048,
        1 << 20,
    )


def own_part(table, a_blocks, p_blocks):
    return call(
        own_kernel,
        (table, a_blocks, p_blocks),
        1,
        [
            SHAPE((SEGS + 1, DIM, DIM), F32),
            SHAPE((2 * SLOTS + 1, DIM, DIM), F32),
            SHAPE((HALO_MAX, DIM, DIM), BF16),
            SHAPE((EDGE_MAX, DIM, DIM), BF16),
        ],
        [VMEM] * 4,
        [
            pltpu.VMEM((ROWS * SLOTS, DIM, DIM), BF16),
            pltpu.VMEM((SEGS + 2 * SLOTS + 2, DIM, DIM), F32),
        ],
        128,
        8 << 20,
    )


def edge_part(table, edge_acc, left_edge, sources):
    return call(
        edge_kernel,
        (table, edge_acc, left_edge, *sources),
        1,
        [SHAPE((SLOTS, DIM, DIM), BF16)] * 3,
        [VMEM] * 3,
        [pltpu.VMEM((2 * SLOTS + 1, DIM, DIM), F32)],
        8,
        2 << 20,
    )


def halo_part(table, acc, left_halo, sources):
    return call(
        halo_kernel,
        (table, acc, left_halo, *sources),
        1,
        [SHAPE((2 * SLOTS, DIM, DIM), F32), SHAPE((COARSE, SLOTS, DIM, DIM), BF16)],
        [VMEM, ANY],
        [
            pltpu.VMEM((SEGS + 1, DIM, DIM), F32),
            pltpu.VMEM((COARSE - 2, SLOTS, DIM, DIM), BF16),
            pltpu.SemaphoreType.DMA(()),
        ],
        32,
        6 << 20,
    )


def last_part(acc, got, out):
    return call(
        last_kernel,
        (acc, *got, out),
        0,
        SHAPE((COARSE, SLOTS, DIM, DIM), BF16),
        ANY,
        [pltpu.VMEM((2, SLOTS, DIM, DIM), BF16), pltpu.SemaphoreType.DMA((2,))],
        1,
        2 << 20,
        1,
        {4: 0},
    )


def body(a_blocks, p_blocks, a_cols, a_target, agg, refine):
    count = lax.axis_size(AXES)
    pairs = [[], [], []]
    for i in range(count - 1):
        pairs[color_of(i)] += [(i, i + 1), (i + 1, i)]
    ints = jnp.concatenate([a_cols.T, a_target.T, agg[None], refine[None]])

    from_0 = lax.ppermute(p_blocks, AXES, pairs[0])
    table = list_part(ints)
    from_1 = lax.ppermute(p_blocks, AXES, pairs[1])
    from_2 = lax.ppermute(p_blocks, AXES, pairs[2])
    sources = (from_0, from_1, from_2)
    acc, edge_acc, left_halo, left_edge = own_part(table, a_blocks, p_blocks)
    msg_0, msg_1, msg_2 = edge_part(table, edge_acc, left_edge, sources)
    got = [lax.ppermute(msg, AXES, pairs[color]) for color, msg in ((0, msg_0), (1, msg_1), (2, msg_2))]
    acc, out = halo_part(table, acc, left_halo, sources)
    return last_part(acc, got, out)


def solution(mesh):
    return jax.shard_map(
        body,
        mesh=mesh,
        in_specs=(
            P(AXES, None, None, None),
            P(AXES, None, None),
            P(AXES, None),
            P(AXES, None),
            P(AXES),
            P(AXES),
        ),
        out_specs=P(AXES, None, None, None),
        check_vma=False,
    )
```

time: 42 us -> 39.1 us (0.931)
  waiting for transfers between devices: 6.11 us -> 3.25 us
  local copies, waits for them, and re-layouts: 1.04 us -> 0.01 us
  Pallas kernels: 10.5 us -> 11.1 us
    ppermute x4 -> x6, waiting for transfers between devices: 6.11 us -> 3.25 us  [the longest x3 2.54 us: body(): lax.ppermute(msg, AXES, pairs[color])]
    unnamed x4, local copies, waits for them, and re-layouts: 1.04 us -> 0.01 us
    pallas_call x5, Pallas kernels: 10.5 us -> 11.1 us  [call(): pl.pallas_call(kernel, out_shape=outs, in_specs=[SMEM] * smems + [VMEM] *...]
    ppermute x4 -> x6, starting transfers between devices: 23.3 us -> 23.6 us  [the longest x1 10.8 us: body(): from_1 = lax.ppermute(p_blocks, AXES, pairs[1])]
  transfers between devices with their start and end apart: 4 -> 6, of which waited for: 3 -> 2; matrix products, arithmetic and copies ran while one was open for 2% -> 2% of each run, Pallas kernels for 19% -> 24%
where the time goes in v3:
time: 39.1 us; the launch traced here: 38.8 us
  starting transfers between devices  23.6 us (60%)
  Pallas kernels  11.1 us (28%)
  waiting for transfers between devices  3.25 us (8%)
  other arithmetic  0.75 us (2%)
    pallas_call x5, Pallas kernels, call(): pl.pallas_call(kernel, out_shape=outs, in_specs=[SMEM] * smems + [VMEM] *...  11.1 us
    ppermute x1, starting transfers between devices, body(): from_1 = lax.ppermute(p_blocks, AXES, pairs[1])  10.8 us
    ppermute x3, starting transfers between devices, body(): lax.ppermute(msg, AXES, pairs[color])  8.63 us
    ppermute x1, starting transfers between devices, body(): from_0 = lax.ppermute(p_blocks, AXES, pairs[0])  3.47 us
    ppermute x3, waiting for transfers between devices, body(): lax.ppermute(msg, AXES, pairs[color])  2.54 us
  transfers between devices with their start and end apart: 6, of which 2 were waited for; matrix products, arithmetic and copies ran while one was open for 2% of the time, Pallas kernels for 24%

profile of v3, /device:TPU:6, one launch (start us, length us, event | category | flops | bytes accessed | tf_op | source)
XLA Modules:
  0.0 38.8 jit_solution(12604117607398544142)
XLA Ops:
  0.0 3.5 %collective-permute-start = (bf16[16,128,128]{2,1,0:T(8,128)(2,1)}, bf16[16,128,128]{2,1,0:T(8,128)(2,1)S(1)}, u32[]{:S(2)}, u32[]{:S(2)}) collective-permute-start(bf16[16,128,128]{2,1,0:T(8,128)(2,1)} %p.1), channel_id=1, source_target_pairs={{0,1},{1,0},{2,3},{3,2},{4,5},{5,4},{6,7},{7,6},{8,9},{9,8},{10,11... | collective-permute-start | bytes 1572872 | tf_op jit(solution)/shard_map/ppermute | solution.py:271
  3.5 10.8 %collective-permute-start.1 = (bf16[16,128,128]{2,1,0:T(8,128)(2,1)}, bf16[16,128,128]{2,1,0:T(8,128)(2,1)S(1)}, u32[]{:S(2)}, u32[]{:S(2)}) collective-permute-start(bf16[16,128,128]{2,1,0:T(8,128)(2,1)} %p.1), channel_id=1, source_target_pairs={{1,2},{2,1},{3,4},{4,3},{5,6},{6,5},{7,8},{8,7},{9,10},{10,9},{11,... | collective-permute-start | bytes 1572872 | tf_op jit(solution)/shard_map/ppermute | solution.py:273
  14.3 0.7 %collective-permute-start.2 = (bf16[16,128,128]{2,1,0:T(8,128)(2,1)}, bf16[16,128,128]{2,1,0:T(8,128)(2,1)S(1)}, u32[]{:S(2)}, u32[]{:S(2)}) collective-permute-start(bf16[16,128,128]{2,1,0:T(8,128)(2,1)} %p.1), channel_id=1, source_target_pairs={{126,127},{127,126},{254,255},{255,254},{382,383},{383,382},{510,5... | collective-permute-start | bytes 1572872 | tf_op jit(solution)/shard_map/ppermute | solution.py:274
  15.0 0.7 %pad_add_fusion.ints = s32[16,16]{1,0:T(8,128)S(1)} fusion(s32[1,16]{1,0:T(1,128)} %bitcast.6, s32[1,16]{1,0:T(1,128)} %bitcast.7, s32[7,16]{1,0:T(8,128)} %bitcast.4, s32[7,16]{1,0:T(8,128)} %bitcast.5), kind=kLoop, calls=%fused_computation | loop fusion | flops 768 | bytes 2048 | tf_op jit(solution)/shard_map/concatenate | solution.py:269
  15.7 0.0 copy-start
  15.7 0.0 copy-start.1
  15.7 2.9 %shard_map.64.table = s32[400]{0:T(512)S(1)} custom-call(s32[16,16]{1,0:T(8,128)S(1)} %pad_add_fusion.ints), custom_call_target="tpu_custom_call" | custom-call | flops 8589934592 | bytes 1048576 | tf_op jit(solution)/shard_map/pallas_call | solution.py:173
  18.6 0.0 copy-done
  18.6 0.0 copy-done.1
  18.7 4.1 %shard_map.65 = (f32[29,128,128]{2,1,0:T(8,128)S(1)}, f32[15,128,128]{2,1,0:T(8,128)S(1)}, bf16[72,128,128]{2,1,0:T(8,128)(2,1)S(1)}, bf16[24,128,128]{2,1,0:T(8,128)(2,1)S(1)}) custom-call(s32[400]{0:T(512)S(1)} %shard_map.64.table, bf16[16,7,128,128]{3,2,1,0:T(8,128)(2,1)S(1)} %copy-done, bf16[16,128,128]{2,1,0:T(8,128)(2,1)S(1)} %copy-done.1), custom_call_target="tpu_custom_call" | custom-call | flops 536870912 | bytes 8388608 | tf_op jit(solution)/shard_map/pallas_call | solution.py:173
  22.7 0.0 collective-permute-done.from_0
  22.7 0.7 %collective-permute-done.1.from_1 = bf16[16,128,128]{2,1,0:T(8,128)(2,1)S(1)} collective-permute-done((bf16[16,128,128]{2,1,0:T(8,128)(2,1)}, bf16[16,128,128]{2,1,0:T(8,128)(2,1)S(1)}, u32[]{:S(2)}, u32[]{:S(2)}) %collective-permute-start.1) | collective-permute-done | bytes 524320 | tf_op jit(solution)/shard_map/ppermute | solution.py:273
  23.4 0.0 collective-permute-done.2.from_2
  23.5 1.0 %shard_map.67 = (bf16[7,128,128]{2,1,0:T(8,128)(2,1)S(1)}, bf16[7,128,128]{2,1,0:T(8,128)(2,1)S(1)}, bf16[7,128,128]{2,1,0:T(8,128)(2,1)S(1)}) custom-call(s32[400]{0:T(512)S(1)} %shard_map.64.table, f32[15,128,128]{2,1,0:T(8,128)S(1)} %get-tuple-element.17.edge_acc, bf16[24,128,128]{2,1,0:T(8,128)(2,1)S(1)} %get-tuple-element.18.left_edge, ...), custom_call_target="tpu_custom_call" | custom-call | flops 33554432 | bytes 2097152 | tf_op jit(solution)/shard_map/pallas_call | solution.py:173
  24.4 1.9 %collective-permute-start.3 = (bf16[7,128,128]{2,1,0:T(8,128)(2,1)S(1)}, bf16[7,128,128]{2,1,0:T(8,128)(2,1)S(1)}, u32[]{:S(2)}, u32[]{:S(2)}) collective-permute-start(bf16[7,128,128]{2,1,0:T(8,128)(2,1)S(1)} %get-tuple-element.19), channel_id=1, source_target_pairs={{0,1},{1,0},{2,3},{3,2},{4,5},{5,4},{6,7},{7,6},{8,9},{9,8},{10,11... | collective-permute-start | bytes 688136 | tf_op jit(solution)/shard_map/ppermute | solution.py:278
  26.3 6.0 %collective-permute-start.4 = (bf16[7,128,128]{2,1,0:T(8,128)(2,1)S(1)}, bf16[7,128,128]{2,1,0:T(8,128)(2,1)S(1)}, u32[]{:S(2)}, u32[]{:S(2)}) collective-permute-start(bf16[7,128,128]{2,1,0:T(8,128)(2,1)S(1)} %get-tuple-element.20), channel_id=1, source_target_pairs={{1,2},{2,1},{3,4},{4,3},{5,6},{6,5},{7,8},{8,7},{9,10},{10,9},{11,... | collective-permute-start | bytes 688136 | tf_op jit(solution)/shard_map/ppermute | solution.py:278
  32.4 0.7 %collective-permute-start.5 = (bf16[7,128,128]{2,1,0:T(8,128)(2,1)S(1)}, bf16[7,128,128]{2,1,0:T(8,128)(2,1)S(1)}, u32[]{:S(2)}, u32[]{:S(2)}) collective-permute-start(bf16[7,128,128]{2,1,0:T(8,128)(2,1)S(1)} %get-tuple-element.21), channel_id=1, source_target_pairs={{126,127},{127,126},{254,255},{255,254},{382,383},{383,382},{510,5... | collective-permute-start | bytes 688136 | tf_op jit(solution)/shard_map/ppermute | solution.py:278
  33.1 2.3 %shard_map.66 = (f32[14,128,128]{2,1,0:T(8,128)S(1)}, bf16[4,7,128,128]{3,2,1,0:T(8,128)(2,1)}) custom-call(s32[400]{0:T(512)S(1)} %shard_map.64.table, f32[29,128,128]{2,1,0:T(8,128)S(1)} %get-tuple-element.14.acc_in, bf16[72,128,128]{2,1,0:T(8,128)(2,1)S(1)} %get-tuple-element.15.left_halo, bf16[16,128,128]{2,1,0:T(8,128)(2,1)S(1)} %collective-permute-done.from_0, ...), custom_call_target="tpu_custom_call" | custom-call | flops 134217728 | bytes 6291456 | tf_op jit(solution)/shard_map/pallas_call | solution.py:173
  35.4 0.0 collective-permute-done.3.got_0
  35.4 2.5 %collective-permute-done.4.got_1 = bf16[7,128,128]{2,1,0:T(8,128)(2,1)S(1)} collective-permute-done((bf16[7,128,128]{2,1,0:T(8,128)(2,1)S(1)}, bf16[7,128,128]{2,1,0:T(8,128)(2,1)S(1)}, u32[]{:S(2)}, u32[]{:S(2)}) %collective-permute-start.4) | collective-permute-done | bytes 229408 | tf_op jit(solution)/shard_map/ppermute | solution.py:278
  37.9 0.0 collective-permute-done.5.got_2
  37.9 0.9 %shard_map.68 = bf16[4,7,128,128]{3,2,1,0:T(8,128)(2,1)} custom-call(f32[14,128,128]{2,1,0:T(8,128)S(1)} %get-tuple-element.16.acc, bf16[7,128,128]{2,1,0:T(8,128)(2,1)S(1)} %collective-permute-done.3.got_0, bf16[7,128,128]{2,1,0:T(8,128)(2,1)S(1)} %collective-permute-done.4.got_1, ...), custom_call_target="tpu_custom_call", output_to_operand_aliasing={{}: (4, {})} | custom-call | flops 4194304 | bytes 2097152 | tf_op jit(solution)/shard_map/pallas_call | solution.py:173
Async XLA Ops:
  0.0 22.7 %collective-permute-start = (bf16[16,128,128]{2,1,0:T(8,128)(2,1)}, bf16[16,128,128]{2,1,0:T(8,128)(2,1)S(1)}, u32[]{:S(2)}, u32[]{:S(2)}) collective-permute-start(bf16[16,128,128]{2,1,0:T(8,128)(2,1)} %p.1), channel_id=1, source_target_pairs={{0,1},{1,0},{2,3},{3,2},{4,5},{5,4},{6,7},{7,6},{8,9},{9,8},{10,11... | collective-permute-start | bytes 1572872 | tf_op jit(solution)/shard_map/ppermute | solution.py:271
  3.5 20.0 %collective-permute-start.1 = (bf16[16,128,128]{2,1,0:T(8,128)(2,1)}, bf16[16,128,128]{2,1,0:T(8,128)(2,1)S(1)}, u32[]{:S(2)}, u32[]{:S(2)}) collective-permute-start(bf16[16,128,128]{2,1,0:T(8,128)(2,1)} %p.1), channel_id=1, source_target_pairs={{1,2},{2,1},{3,4},{4,3},{5,6},{6,5},{7,8},{8,7},{9,10},{10,9},{11,... | collective-permute-start | bytes 1572872 | tf_op jit(solution)/shard_map/ppermute | solution.py:273
  14.3 9.2 %collective-permute-start.2 = (bf16[16,128,128]{2,1,0:T(8,128)(2,1)}, bf16[16,128,128]{2,1,0:T(8,128)(2,1)S(1)}, u32[]{:S(2)}, u32[]{:S(2)}) collective-permute-start(bf16[16,128,128]{2,1,0:T(8,128)(2,1)} %p.1), channel_id=1, source_target_pairs={{126,127},{127,126},{254,255},{255,254},{382,383},{383,382},{510,5... | collective-permute-start | bytes 1572872 | tf_op jit(solution)/shard_map/ppermute | solution.py:274
  15.7 2.9 %copy-start = (bf16[16,7,128,128]{3,2,1,0:T(8,128)(2,1)S(1)}, bf16[16,7,128,128]{3,2,1,0:T(8,128)(2,1)}, u32[]{:S(2)}) copy-start(bf16[16,7,128,128]{3,2,1,0:T(8,128)(2,1)} %a.1) | copy-start | bytes 11010052
  15.7 2.9 %copy-start.1 = (bf16[16,128,128]{2,1,0:T(8,128)(2,1)S(1)}, bf16[16,128,128]{2,1,0:T(8,128)(2,1)}, u32[]{:S(2)}) copy-start(bf16[16,128,128]{2,1,0:T(8,128)(2,1)} %p.1) | copy-start | bytes 1572868
  24.4 10.9 %collective-permute-start.3 = (bf16[7,128,128]{2,1,0:T(8,128)(2,1)S(1)}, bf16[7,128,128]{2,1,0:T(8,128)(2,1)S(1)}, u32[]{:S(2)}, u32[]{:S(2)}) collective-permute-start(bf16[7,128,128]{2,1,0:T(8,128)(2,1)S(1)} %get-tuple-element.19), channel_id=1, source_target_pairs={{0,1},{1,0},{2,3},{3,2},{4,5},{5,4},{6,7},{7,6},{8,9},{9,8},{10,11... | collective-permute-start | bytes 688136 | tf_op jit(solution)/shard_map/ppermute | solution.py:278
  26.3 11.6 %collective-permute-start.4 = (bf16[7,128,128]{2,1,0:T(8,128)(2,1)S(1)}, bf16[7,128,128]{2,1,0:T(8,128)(2,1)S(1)}, u32[]{:S(2)}, u32[]{:S(2)}) collective-permute-start(bf16[7,128,128]{2,1,0:T(8,128)(2,1)S(1)} %get-tuple-element.20), channel_id=1, source_target_pairs={{1,2},{2,1},{3,4},{4,3},{5,6},{6,5},{7,8},{8,7},{9,10},{10,9},{11,... | collective-permute-start | bytes 688136 | tf_op jit(solution)/shard_map/ppermute | solution.py:278
  32.4 5.5 %collective-permute-start.5 = (bf16[7,128,128]{2,1,0:T(8,128)(2,1)S(1)}, bf16[7,128,128]{2,1,0:T(8,128)(2,1)S(1)}, u32[]{:S(2)}, u32[]{:S(2)}) collective-permute-start(bf16[7,128,128]{2,1,0:T(8,128)(2,1)S(1)} %get-tuple-element.21), channel_id=1, source_target_pairs={{126,127},{127,126},{254,255},{255,254},{382,383},{383,382},{510,5... | collective-permute-start | bytes 688136 | tf_op jit(solution)/shard_map/ppermute | solution.py:278

commit v4 on v3

--- a/solution.py
+++ b/solution.py
@@ -133,13 +133,12 @@
     return right
 
 
-def edge_kernel(table, edge_acc, left_edge, from_0, from_1, from_2, msg_0, msg_1, msg_2, total):
+def edge_kernel(table, edge_acc, left_edge, from_0, from_1, from_2, msg_up, msg_down, total):
     total[...] = edge_acc[...]
     add_items(table[COUNTS + 1], table, EDGE, left_edge, picker(table, (from_0, from_1, from_2)), total, False)
-    for color, msg in enumerate((msg_0, msg_1, msg_2)):
-        side = jnp.where(table[COUNTS + 4] == color, SLOTS, 0)
-        for s in range(SLOTS):
-            msg[s] = total[side + s].astype(BF16)
+    for s in range(SLOTS):
+        msg_down[s] = total[s].astype(BF16)
+        msg_up[s] = total[SLOTS + s].astype(BF16)
 
 
 def halo_kernel(table, acc_in, left_halo, from_0, from_1, from_2, acc, out, total, inner, sem):
@@ -154,15 +153,11 @@
     copy.wait()
 
 
-def last_kernel(acc, got_0, got_1, got_2, out_in, out, outer, sems):
-    got = (got_0, got_1, got_2)
-    device = lax.axis_index(AXES[0]) * lax.axis_size(AXES[1]) + lax.axis_index(AXES[1])
+def last_kernel(acc, from_before, from_after, out_in, out, outer, sems):
     copies = []
-    for side, row in enumerate((0, COARSE - 1)):
-        color = color_in_kernel(device - 1 + side)
+    for side, (row, got) in enumerate(((0, from_before), (COARSE - 1, from_after))):
         for s in range(SLOTS):
-            value = acc[side * SLOTS + s] + choose(color, [g[s] for g in got]).astype(F32)
-            outer[side, s] = value.astype(BF16)
+            outer[side, s] = (acc[side * SLOTS + s] + got[s].astype(F32)).astype(BF16)
         copies.append(pltpu.make_async_copy(outer.at[side], out.at[row], sems.at[side]))
         copies[-1].start()
     for copy in copies:
@@ -221,8 +216,8 @@
         edge_kernel,
         (table, edge_acc, left_edge, *sources),
         1,
-        [SHAPE((SLOTS, DIM, DIM), BF16)] * 3,
-        [VMEM] * 3,
+        [SHAPE((SLOTS, DIM, DIM), BF16)] * 2,
+        [VMEM] * 2,
         [pltpu.VMEM((2 * SLOTS + 1, DIM, DIM), F32)],
         8,
         2 << 20,
@@ -257,7 +252,7 @@
         1,
         2 << 20,
         1,
-        {4: 0},
+        {3: 0},
     )
 
 
@@ -274,8 +269,10 @@
     from_2 = lax.ppermute(p_blocks, AXES, pairs[2])
     sources = (from_0, from_1, from_2)
     acc, edge_acc, left_halo, left_edge = own_part(table, a_blocks, p_blocks)
-    msg_0, msg_1, msg_2 = edge_part(table, edge_acc, left_edge, sources)
-    got = [lax.ppermute(msg, AXES, pairs[color]) for color, msg in ((0, msg_0), (1, msg_1), (2, msg_2))]
+    msg_up, msg_down = edge_part(table, edge_acc, left_edge, sources)
+    up = [(i, i + 1) for i in range(count - 1)]
+    down = [(j, i) for i, j in up]
+    got = [lax.ppermute(msg_up, AXES, up), lax.ppermute(msg_down, AXES, down)]
     acc, out = halo_part(table, acc, left_halo, sources)
     return last_part(acc, got, out)
 

time: 39.1 us -> 38.8 us (level)
  Pallas kernels: 11.1 us -> 10 us
  starting transfers between devices: 23.6 us -> 24.7 us
    ppermute x3 -> x2, starting transfers between devices: 8.63 us -> 9.78 us  [body(): got = [lax.ppermute(msg_up, AXES, up), lax.ppermute(msg_down, AXES, down)]]
    pallas_call x5, Pallas kernels: 11.1 us -> 10 us  [call(): pl.pallas_call(kernel, out_shape=outs, in_specs=[SMEM] * smems + [VMEM] *...]
    ppermute x3 -> x2, waiting for transfers between devices: 2.54 us -> 1.47 us  [body(): got = [lax.ppermute(msg_up, AXES, up), lax.ppermute(msg_down, AXES, down)]]
    ppermute x1, waiting for transfers between devices: 0.71 us -> 1.45 us  [body(): from_1 = lax.ppermute(p_blocks, AXES, pairs[1])]
  transfers between devices with their start and end apart: 6 -> 5, of which waited for: 2 -> 2; matrix products, arithmetic and copies ran while one was open for 2% -> 2% of each run, Pallas kernels for 24% -> 21%
where the time goes in v4:
time: 38.8 us; the launch traced here: 38.5 us
  starting transfers between devices  24.7 us (64%)
  Pallas kernels  10 us (26%)
  waiting for transfers between devices  2.93 us (8%)
  other arithmetic  0.75 us (2%)
    ppermute x1, starting transfers between devices, body(): from_1 = lax.ppermute(p_blocks, AXES, pairs[1])  10.8 us
    pallas_call x5, Pallas kernels, call(): pl.pallas_call(kernel, out_shape=outs, in_specs=[SMEM] * smems + [VMEM] *...  10 us
    ppermute x2, starting transfers between devices, body(): got = [lax.ppermute(msg_up, AXES, up), lax.ppermute(msg_down, AXES, down)]  9.78 us
    ppermute x1, starting transfers between devices, body(): from_0 = lax.ppermute(p_blocks, AXES, pairs[0])  3.47 us
    ppermute x2, waiting for transfers between devices, body(): got = [lax.ppermute(msg_up, AXES, up), lax.ppermute(msg_down, AXES, down)]  1.47 us
    ppermute x1, waiting for transfers between devices, body(): from_1 = lax.ppermute(p_blocks, AXES, pairs[1])  1.45 us
  transfers between devices with their start and end apart: 5, of which 2 were waited for; matrix products, arithmetic and copies ran while one was open for 2% of the time, Pallas kernels for 21%

profile of v4, /device:TPU:6, one launch (start us, length us, event | category | flops | bytes accessed | tf_op | source)
XLA Modules:
  0.0 38.5 jit_solution(6069542346376969725)
XLA Ops:
  0.0 3.5 %collective-permute-start = (bf16[16,128,128]{2,1,0:T(8,128)(2,1)}, bf16[16,128,128]{2,1,0:T(8,128)(2,1)S(1)}, u32[]{:S(2)}, u32[]{:S(2)}) collective-permute-start(bf16[16,128,128]{2,1,0:T(8,128)(2,1)} %p.1), channel_id=1, source_target_pairs={{0,1},{1,0},{2,3},{3,2},{4,5},{5,4},{6,7},{7,6},{8,9},{9,8},{10,11... | collective-permute-start | bytes 1572872 | tf_op jit(solution)/shard_map/ppermute | solution.py:266
  3.5 10.8 %collective-permute-start.1 = (bf16[16,128,128]{2,1,0:T(8,128)(2,1)}, bf16[16,128,128]{2,1,0:T(8,128)(2,1)S(1)}, u32[]{:S(2)}, u32[]{:S(2)}) collective-permute-start(bf16[16,128,128]{2,1,0:T(8,128)(2,1)} %p.1), channel_id=1, source_target_pairs={{1,2},{2,1},{3,4},{4,3},{5,6},{6,5},{7,8},{8,7},{9,10},{10,9},{11,... | collective-permute-start | bytes 1572872 | tf_op jit(solution)/shard_map/ppermute | solution.py:268
  14.3 0.7 %collective-permute-start.2 = (bf16[16,128,128]{2,1,0:T(8,128)(2,1)}, bf16[16,128,128]{2,1,0:T(8,128)(2,1)S(1)}, u32[]{:S(2)}, u32[]{:S(2)}) collective-permute-start(bf16[16,128,128]{2,1,0:T(8,128)(2,1)} %p.1), channel_id=1, source_target_pairs={{126,127},{127,126},{254,255},{255,254},{382,383},{383,382},{510,5... | collective-permute-start | bytes 1572872 | tf_op jit(solution)/shard_map/ppermute | solution.py:269
  15.0 0.7 %pad_add_fusion.ints = s32[16,16]{1,0:T(8,128)S(1)} fusion(s32[1,16]{1,0:T(1,128)} %bitcast.6, s32[1,16]{1,0:T(1,128)} %bitcast.7, s32[7,16]{1,0:T(8,128)} %bitcast.4, s32[7,16]{1,0:T(8,128)} %bitcast.5), kind=kLoop, calls=%fused_computation | loop fusion | flops 768 | bytes 2048 | tf_op jit(solution)/shard_map/concatenate | solution.py:264
  15.7 0.0 copy-start
  15.7 0.0 copy-start.1
  15.7 2.9 %shard_map.64.table = s32[400]{0:T(512)S(1)} custom-call(s32[16,16]{1,0:T(8,128)S(1)} %pad_add_fusion.ints), custom_call_target="tpu_custom_call" | custom-call | flops 8589934592 | bytes 1048576 | tf_op jit(solution)/shard_map/pallas_call | solution.py:168
  18.6 0.0 copy-done
  18.6 0.0 copy-done.1
  18.7 3.3 %shard_map.65 = (f32[29,128,128]{2,1,0:T(8,128)S(1)}, f32[15,128,128]{2,1,0:T(8,128)S(1)}, bf16[72,128,128]{2,1,0:T(8,128)(2,1)S(1)}, bf16[24,128,128]{2,1,0:T(8,128)(2,1)S(1)}) custom-call(s32[400]{0:T(512)S(1)} %shard_map.64.table, bf16[16,7,128,128]{3,2,1,0:T(8,128)(2,1)S(1)} %copy-done, bf16[16,128,128]{2,1,0:T(8,128)(2,1)S(1)} %copy-done.1), custom_call_target="tpu_custom_call" | custom-call | flops 536870912 | bytes 8388608 | tf_op jit(solution)/shard_map/pallas_call | solution.py:168
  22.0 0.0 collective-permute-done.from_0
  22.0 1.5 %collective-permute-done.1.from_1 = bf16[16,128,128]{2,1,0:T(8,128)(2,1)S(1)} collective-permute-done((bf16[16,128,128]{2,1,0:T(8,128)(2,1)}, bf16[16,128,128]{2,1,0:T(8,128)(2,1)S(1)}, u32[]{:S(2)}, u32[]{:S(2)}) %collective-permute-start.1) | collective-permute-done | bytes 524320 | tf_op jit(solution)/shard_map/ppermute | solution.py:268
  23.4 0.0 collective-permute-done.2.from_2
  23.5 0.9 %shard_map.67 = (bf16[7,128,128]{2,1,0:T(8,128)(2,1)S(1)}, bf16[7,128,128]{2,1,0:T(8,128)(2,1)S(1)}) custom-call(s32[400]{0:T(512)S(1)} %shard_map.64.table, f32[15,128,128]{2,1,0:T(8,128)S(1)} %get-tuple-element.16.edge_acc, bf16[24,128,128]{2,1,0:T(8,128)(2,1)S(1)} %get-tuple-element.17.left_edge, bf16[16,128,128]{2,1,0:T(8,128)(2,1)S(1)} %collective-permute-done.from_0, ...), custom_call_target="tpu_custom_call" | custom-call | flops 33554432 | bytes 2097152 | tf_op jit(solution)/shard_map/pallas_call | solution.py:168
  24.4 1.9 %collective-permute-start.3 = (bf16[7,128,128]{2,1,0:T(8,128)(2,1)S(1)}, bf16[7,128,128]{2,1,0:T(8,128)(2,1)S(1)}, u32[]{:S(2)}, u32[]{:S(2)}) collective-permute-start(bf16[7,128,128]{2,1,0:T(8,128)(2,1)S(1)} %get-tuple-element.18), channel_id=1, source_target_pairs={{0,1},{1,2},{2,3},{3,4},{4,5},{5,6},{6,7},{7,8},{8,9},{9,10},{10,1... | collective-permute-start | bytes 688136 | tf_op jit(solution)/shard_map/ppermute | solution.py:275
  26.3 7.9 %collective-permute-start.4 = (bf16[7,128,128]{2,1,0:T(8,128)(2,1)S(1)}, bf16[7,128,128]{2,1,0:T(8,128)(2,1)S(1)}, u32[]{:S(2)}, u32[]{:S(2)}) collective-permute-start(bf16[7,128,128]{2,1,0:T(8,128)(2,1)S(1)} %get-tuple-element.19), channel_id=1, source_target_pairs={{1,0},{2,1},{3,2},{4,3},{5,4},{6,5},{7,6},{8,7},{9,8},{10,9},{11,1... | collective-permute-start | bytes 688136 | tf_op jit(solution)/shard_map/ppermute | solution.py:275
  34.2 2.0 %shard_map.66 = (f32[14,128,128]{2,1,0:T(8,128)S(1)}, bf16[4,7,128,128]{3,2,1,0:T(8,128)(2,1)}) custom-call(s32[400]{0:T(512)S(1)} %shard_map.64.table, f32[29,128,128]{2,1,0:T(8,128)S(1)} %get-tuple-element.13.acc_in, bf16[72,128,128]{2,1,0:T(8,128)(2,1)S(1)} %get-tuple-element.14.left_halo, bf16[16,128,128]{2,1,0:T(8,128)(2,1)S(1)} %collective-permute-done.from_0, ...), custom_call_target="tpu_custom_call" | custom-call | flops 134217728 | bytes 6291456 | tf_op jit(solution)/shard_map/pallas_call | solution.py:168
  36.2 0.0 collective-permute-done.3.from_before
  36.2 1.5 %collective-permute-done.4.from_after = bf16[7,128,128]{2,1,0:T(8,128)(2,1)S(1)} collective-permute-done((bf16[7,128,128]{2,1,0:T(8,128)(2,1)S(1)}, bf16[7,128,128]{2,1,0:T(8,128)(2,1)S(1)}, u32[]{:S(2)}, u32[]{:S(2)}) %collective-permute-start.4) | collective-permute-done | bytes 229408 | tf_op jit(solution)/shard_map/ppermute | solution.py:275
  37.7 0.8 %shard_map.68 = bf16[4,7,128,128]{3,2,1,0:T(8,128)(2,1)} custom-call(f32[14,128,128]{2,1,0:T(8,128)S(1)} %get-tuple-element.15.acc, bf16[7,128,128]{2,1,0:T(8,128)(2,1)S(1)} %collective-permute-done.3.from_before, bf16[7,128,128]{2,1,0:T(8,128)(2,1)S(1)} %collective-permute-done.4.from_after, ...), custom_call_target="tpu_custom_call", output_to_operand_aliasing={{}: (3, {})} | custom-call | flops 4194304 | bytes 2097152 | tf_op jit(solution)/shard_map/pallas_call | solution.py:168
Async XLA Ops:
  0.0 22.0 %collective-permute-start = (bf16[16,128,128]{2,1,0:T(8,128)(2,1)}, bf16[16,128,128]{2,1,0:T(8,128)(2,1)S(1)}, u32[]{:S(2)}, u32[]{:S(2)}) collective-permute-start(bf16[16,128,128]{2,1,0:T(8,128)(2,1)} %p.1), channel_id=1, source_target_pairs={{0,1},{1,0},{2,3},{3,2},{4,5},{5,4},{6,7},{7,6},{8,9},{9,8},{10,11... | collective-permute-start | bytes 1572872 | tf_op jit(solution)/shard_map/ppermute | solution.py:266
  3.5 20.0 %collective-permute-start.1 = (bf16[16,128,128]{2,1,0:T(8,128)(2,1)}, bf16[16,128,128]{2,1,0:T(8,128)(2,1)S(1)}, u32[]{:S(2)}, u32[]{:S(2)}) collective-permute-start(bf16[16,128,128]{2,1,0:T(8,128)(2,1)} %p.1), channel_id=1, source_target_pairs={{1,2},{2,1},{3,4},{4,3},{5,6},{6,5},{7,8},{8,7},{9,10},{10,9},{11,... | collective-permute-start | bytes 1572872 | tf_op jit(solution)/shard_map/ppermute | solution.py:268
  14.3 9.2 %collective-permute-start.2 = (bf16[16,128,128]{2,1,0:T(8,128)(2,1)}, bf16[16,128,128]{2,1,0:T(8,128)(2,1)S(1)}, u32[]{:S(2)}, u32[]{:S(2)}) collective-permute-start(bf16[16,128,128]{2,1,0:T(8,128)(2,1)} %p.1), channel_id=1, source_target_pairs={{126,127},{127,126},{254,255},{255,254},{382,383},{383,382},{510,5... | collective-permute-start | bytes 1572872 | tf_op jit(solution)/shard_map/ppermute | solution.py:269
  15.7 2.9 %copy-start = (bf16[16,7,128,128]{3,2,1,0:T(8,128)(2,1)S(1)}, bf16[16,7,128,128]{3,2,1,0:T(8,128)(2,1)}, u32[]{:S(2)}) copy-start(bf16[16,7,128,128]{3,2,1,0:T(8,128)(2,1)} %a.1) | copy-start | bytes 11010052
  15.7 2.9 %copy-start.1 = (bf16[16,128,128]{2,1,0:T(8,128)(2,1)S(1)}, bf16[16,128,128]{2,1,0:T(8,128)(2,1)}, u32[]{:S(2)}) copy-start(bf16[16,128,128]{2,1,0:T(8,128)(2,1)} %p.1) | copy-start | bytes 1572868
  24.4 11.8 %collective-permute-start.3 = (bf16[7,128,128]{2,1,0:T(8,128)(2,1)S(1)}, bf16[7,128,128]{2,1,0:T(8,128)(2,1)S(1)}, u32[]{:S(2)}, u32[]{:S(2)}) collective-permute-start(bf16[7,128,128]{2,1,0:T(8,128)(2,1)S(1)} %get-tuple-element.18), channel_id=1, source_target_pairs={{0,1},{1,2},{2,3},{3,4},{4,5},{5,6},{6,7},{7,8},{8,9},{9,10},{10,1... | collective-permute-start | bytes 688136 | tf_op jit(solution)/shard_map/ppermute | solution.py:275
  26.3 11.4 %collective-permute-start.4 = (bf16[7,128,128]{2,1,0:T(8,128)(2,1)S(1)}, bf16[7,128,128]{2,1,0:T(8,128)(2,1)S(1)}, u32[]{:S(2)}, u32[]{:S(2)}) collective-permute-start(bf16[7,128,128]{2,1,0:T(8,128)(2,1)S(1)} %get-tuple-element.19), channel_id=1, source_target_pairs={{1,0},{2,1},{3,2},{4,3},{5,4},{6,5},{7,6},{8,7},{9,8},{10,9},{11,1... | collective-permute-start | bytes 688136 | tf_op jit(solution)/shard_map/ppermute | solution.py:275

commit v5 on v4

--- a/solution.py
+++ b/solution.py
@@ -28,22 +28,22 @@
 
 
 def color_of(edge):
-    return 2 if edge % 128 == 126 else edge % 2
+    return 2 if edge % 128 in (119, 126) else edge % 2
 
 
 def color_in_kernel(edge):
-    return jnp.where((edge & 127) == 126, 2, edge & 1)
+    return jnp.where(((edge & 127) == 126) | ((edge & 127) == 119), 2, edge & 1)
 
 
 def dot(x, y):
     return jnp.dot(x, y, preferred_element_type=F32)
 
 
-def add_items(count, table, base, left, right, acc, by_slot):
+def add_items(count, table, base, left, right, acc, by_slot, unroll=UNROLL):
     def step(at, carry):
         parts = []
-        for j in range(UNROLL):
-            n = at * UNROLL + j
+        for j in range(unroll):
+            n = at * unroll + j
             code = table[base + n]
             slot = (code & 127) if by_slot else n
             parts.append((code >> 12, dot(left[slot], right((code >> 7) & 31))))
@@ -51,7 +51,7 @@
             acc[seg] += part
         return carry
 
-    lax.fori_loop(0, (count + UNROLL - 1) // UNROLL, step, 0)
+    lax.fori_loop(0, (count + unroll - 1) // unroll, step, 0)
 
 
 def list_kernel(ints, table):
@@ -135,7 +135,7 @@
 
 def edge_kernel(table, edge_acc, left_edge, from_0, from_1, from_2, msg_up, msg_down, total):
     total[...] = edge_acc[...]
-    add_items(table[COUNTS + 1], table, EDGE, left_edge, picker(table, (from_0, from_1, from_2)), total, False)
+    add_items(table[COUNTS + 1], table, EDGE, left_edge, picker(table, (from_0, from_1, from_2)), total, False, 4)
     for s in range(SLOTS):
         msg_down[s] = total[s].astype(BF16)
         msg_up[s] = total[SLOTS + s].astype(BF16)

time: 38.8 us -> 38.5 us (level); the launches traced: 38.5 us -> 37.7 us
  waiting for transfers between devices: 2.93 us -> 2.24 us
    ppermute x1, waiting for transfers between devices: 1.45 us -> 0.76 us  [body(): from_1 = lax.ppermute(p_blocks, AXES, pairs[1])]
  transfers between devices with their start and end apart: 5 -> 5, of which waited for: 2 -> 2; matrix products, arithmetic and copies ran while one was open for 2% -> 2% of each run, Pallas kernels for 21% -> 22%
where the time goes in v5:
time: 38.5 us; the launch traced here: 37.7 us
  starting transfers between devices  24.8 us (64%)
  Pallas kernels  9.75 us (25%)
  waiting for transfers between devices  2.24 us (6%)
  other arithmetic  0.75 us (2%)
    ppermute x1, starting transfers between devices, body(): from_1 = lax.ppermute(p_blocks, AXES, pairs[1])  10.8 us
    ppermute x2, starting transfers between devices, body(): got = [lax.ppermute(msg_up, AXES, up), lax.ppermute(msg_down, AXES, down)]  9.9 us
    pallas_call x5, Pallas kernels, call(): pl.pallas_call(kernel, out_shape=outs, in_specs=[SMEM] * smems + [VMEM] *...  9.75 us
    ppermute x1, starting transfers between devices, body(): from_0 = lax.ppermute(p_blocks, AXES, pairs[0])  3.47 us
    ppermute x2, waiting for transfers between devices, body(): got = [lax.ppermute(msg_up, AXES, up), lax.ppermute(msg_down, AXES, down)]  1.47 us
  transfers between devices with their start and end apart: 5, of which 2 were waited for; matrix products, arithmetic and copies ran while one was open for 2% of the time, Pallas kernels for 22%

profile of v5, /device:TPU:6, one launch (start us, length us, event | category | flops | bytes accessed | tf_op | source)
XLA Modules:
  0.0 37.7 jit_solution(4414798682801139677)
XLA Ops:
  0.0 3.5 %collective-permute-start = (bf16[16,128,128]{2,1,0:T(8,128)(2,1)}, bf16[16,128,128]{2,1,0:T(8,128)(2,1)S(1)}, u32[]{:S(2)}, u32[]{:S(2)}) collective-permute-start(bf16[16,128,128]{2,1,0:T(8,128)(2,1)} %p.1), channel_id=1, source_target_pairs={{0,1},{1,0},{2,3},{3,2},{4,5},{5,4},{6,7},{7,6},{8,9},{9,8},{10,11... | collective-permute-start | bytes 1572872 | tf_op jit(solution)/shard_map/ppermute | solution.py:266
  3.5 10.8 %collective-permute-start.1 = (bf16[16,128,128]{2,1,0:T(8,128)(2,1)}, bf16[16,128,128]{2,1,0:T(8,128)(2,1)S(1)}, u32[]{:S(2)}, u32[]{:S(2)}) collective-permute-start(bf16[16,128,128]{2,1,0:T(8,128)(2,1)} %p.1), channel_id=1, source_target_pairs={{1,2},{2,1},{3,4},{4,3},{5,6},{6,5},{7,8},{8,7},{9,10},{10,9},{11,... | collective-permute-start | bytes 1572872 | tf_op jit(solution)/shard_map/ppermute | solution.py:268
  14.3 0.7 %collective-permute-start.2 = (bf16[16,128,128]{2,1,0:T(8,128)(2,1)}, bf16[16,128,128]{2,1,0:T(8,128)(2,1)S(1)}, u32[]{:S(2)}, u32[]{:S(2)}) collective-permute-start(bf16[16,128,128]{2,1,0:T(8,128)(2,1)} %p.1), channel_id=1, source_target_pairs={{119,120},{120,119},{126,127},{127,126},{247,248},{248,247},{254,2... | collective-permute-start | bytes 1572872 | tf_op jit(solution)/shard_map/ppermute | solution.py:269
  15.0 0.7 %pad_add_fusion.ints = s32[16,16]{1,0:T(8,128)S(1)} fusion(s32[1,16]{1,0:T(1,128)} %bitcast.6, s32[1,16]{1,0:T(1,128)} %bitcast.7, s32[7,16]{1,0:T(8,128)} %bitcast.4, s32[7,16]{1,0:T(8,128)} %bitcast.5), kind=kLoop, calls=%fused_computation | loop fusion | flops 768 | bytes 2048 | tf_op jit(solution)/shard_map/concatenate | solution.py:264
  15.7 0.0 copy-start
  15.7 0.0 copy-start.1
  15.7 2.9 %shard_map.64.table = s32[400]{0:T(512)S(1)} custom-call(s32[16,16]{1,0:T(8,128)S(1)} %pad_add_fusion.ints), custom_call_target="tpu_custom_call" | custom-call | flops 8589934592 | bytes 1048576 | tf_op jit(solution)/shard_map/pallas_call | solution.py:168
  18.6 0.0 copy-done
  18.7 0.0 copy-done.1
  18.7 3.3 %shard_map.65 = (f32[29,128,128]{2,1,0:T(8,128)S(1)}, f32[15,128,128]{2,1,0:T(8,128)S(1)}, bf16[72,128,128]{2,1,0:T(8,128)(2,1)S(1)}, bf16[24,128,128]{2,1,0:T(8,128)(2,1)S(1)}) custom-call(s32[400]{0:T(512)S(1)} %shard_map.64.table, bf16[16,7,128,128]{3,2,1,0:T(8,128)(2,1)S(1)} %copy-done, bf16[16,128,128]{2,1,0:T(8,128)(2,1)S(1)} %copy-done.1), custom_call_target="tpu_custom_call" | custom-call | flops 536870912 | bytes 8388608 | tf_op jit(solution)/shard_map/pallas_call | solution.py:168
  22.0 0.0 collective-permute-done.from_0
  22.0 0.8 %collective-permute-done.1.from_1 = bf16[16,128,128]{2,1,0:T(8,128)(2,1)S(1)} collective-permute-done((bf16[16,128,128]{2,1,0:T(8,128)(2,1)}, bf16[16,128,128]{2,1,0:T(8,128)(2,1)S(1)}, u32[]{:S(2)}, u32[]{:S(2)}) %collective-permute-start.1) | collective-permute-done | bytes 524320 | tf_op jit(solution)/shard_map/ppermute | solution.py:268
  22.7 0.0 collective-permute-done.2.from_2
  22.7 0.7 %shard_map.67 = (bf16[7,128,128]{2,1,0:T(8,128)(2,1)S(1)}, bf16[7,128,128]{2,1,0:T(8,128)(2,1)S(1)}) custom-call(s32[400]{0:T(512)S(1)} %shard_map.64.table, f32[15,128,128]{2,1,0:T(8,128)S(1)} %get-tuple-element.16.edge_acc, bf16[24,128,128]{2,1,0:T(8,128)(2,1)S(1)} %get-tuple-element.17.left_edge, bf16[16,128,128]{2,1,0:T(8,128)(2,1)S(1)} %collective-permute-done.from_0, ...), custom_call_target="tpu_custom_call" | custom-call | flops 33554432 | bytes 2097152 | tf_op jit(solution)/shard_map/pallas_call | solution.py:168
  23.4 1.9 %collective-permute-start.3 = (bf16[7,128,128]{2,1,0:T(8,128)(2,1)S(1)}, bf16[7,128,128]{2,1,0:T(8,128)(2,1)S(1)}, u32[]{:S(2)}, u32[]{:S(2)}) collective-permute-start(bf16[7,128,128]{2,1,0:T(8,128)(2,1)S(1)} %get-tuple-element.18), channel_id=1, source_target_pairs={{0,1},{1,2},{2,3},{3,4},{4,5},{5,6},{6,7},{7,8},{8,9},{9,10},{10,1... | collective-permute-start | bytes 688136 | tf_op jit(solution)/shard_map/ppermute | solution.py:275
  25.4 8.0 %collective-permute-start.4 = (bf16[7,128,128]{2,1,0:T(8,128)(2,1)S(1)}, bf16[7,128,128]{2,1,0:T(8,128)(2,1)S(1)}, u32[]{:S(2)}, u32[]{:S(2)}) collective-permute-start(bf16[7,128,128]{2,1,0:T(8,128)(2,1)S(1)} %get-tuple-element.19), channel_id=1, source_target_pairs={{1,0},{2,1},{3,2},{4,3},{5,4},{6,5},{7,6},{8,7},{9,8},{10,9},{11,1... | collective-permute-start | bytes 688136 | tf_op jit(solution)/shard_map/ppermute | solution.py:275
  33.4 2.0 %shard_map.66 = (f32[14,128,128]{2,1,0:T(8,128)S(1)}, bf16[4,7,128,128]{3,2,1,0:T(8,128)(2,1)}) custom-call(s32[400]{0:T(512)S(1)} %shard_map.64.table, f32[29,128,128]{2,1,0:T(8,128)S(1)} %get-tuple-element.13.acc_in, bf16[72,128,128]{2,1,0:T(8,128)(2,1)S(1)} %get-tuple-element.14.left_halo, bf16[16,128,128]{2,1,0:T(8,128)(2,1)S(1)} %collective-permute-done.from_0, ...), custom_call_target="tpu_custom_call" | custom-call | flops 134217728 | bytes 6291456 | tf_op jit(solution)/shard_map/pallas_call | solution.py:168
  35.4 0.0 collective-permute-done.3.from_before
  35.4 1.5 %collective-permute-done.4.from_after = bf16[7,128,128]{2,1,0:T(8,128)(2,1)S(1)} collective-permute-done((bf16[7,128,128]{2,1,0:T(8,128)(2,1)S(1)}, bf16[7,128,128]{2,1,0:T(8,128)(2,1)S(1)}, u32[]{:S(2)}, u32[]{:S(2)}) %collective-permute-start.4) | collective-permute-done | bytes 229408 | tf_op jit(solution)/shard_map/ppermute | solution.py:275
  36.9 0.8 %shard_map.68 = bf16[4,7,128,128]{3,2,1,0:T(8,128)(2,1)} custom-call(f32[14,128,128]{2,1,0:T(8,128)S(1)} %get-tuple-element.15.acc, bf16[7,128,128]{2,1,0:T(8,128)(2,1)S(1)} %collective-permute-done.3.from_before, bf16[7,128,128]{2,1,0:T(8,128)(2,1)S(1)} %collective-permute-done.4.from_after, ...), custom_call_target="tpu_custom_call", output_to_operand_aliasing={{}: (3, {})} | custom-call | flops 4194304 | bytes 2097152 | tf_op jit(solution)/shard_map/pallas_call | solution.py:168
Async XLA Ops:
  0.0 22.0 %collective-permute-start = (bf16[16,128,128]{2,1,0:T(8,128)(2,1)}, bf16[16,128,128]{2,1,0:T(8,128)(2,1)S(1)}, u32[]{:S(2)}, u32[]{:S(2)}) collective-permute-start(bf16[16,128,128]{2,1,0:T(8,128)(2,1)} %p.1), channel_id=1, source_target_pairs={{0,1},{1,0},{2,3},{3,2},{4,5},{5,4},{6,7},{7,6},{8,9},{9,8},{10,11... | collective-permute-start | bytes 1572872 | tf_op jit(solution)/shard_map/ppermute | solution.py:266
  3.5 19.3 %collective-permute-start.1 = (bf16[16,128,128]{2,1,0:T(8,128)(2,1)}, bf16[16,128,128]{2,1,0:T(8,128)(2,1)S(1)}, u32[]{:S(2)}, u32[]{:S(2)}) collective-permute-start(bf16[16,128,128]{2,1,0:T(8,128)(2,1)} %p.1), channel_id=1, source_target_pairs={{1,2},{2,1},{3,4},{4,3},{5,6},{6,5},{7,8},{8,7},{9,10},{10,9},{11,... | collective-permute-start | bytes 1572872 | tf_op jit(solution)/shard_map/ppermute | solution.py:268
  14.3 8.5 %collective-permute-start.2 = (bf16[16,128,128]{2,1,0:T(8,128)(2,1)}, bf16[16,128,128]{2,1,0:T(8,128)(2,1)S(1)}, u32[]{:S(2)}, u32[]{:S(2)}) collective-permute-start(bf16[16,128,128]{2,1,0:T(8,128)(2,1)} %p.1), channel_id=1, source_target_pairs={{119,120},{120,119},{126,127},{127,126},{247,248},{248,247},{254,2... | collective-permute-start | bytes 1572872 | tf_op jit(solution)/shard_map/ppermute | solution.py:269
  15.7 2.9 %copy-start = (bf16[16,7,128,128]{3,2,1,0:T(8,128)(2,1)S(1)}, bf16[16,7,128,128]{3,2,1,0:T(8,128)(2,1)}, u32[]{:S(2)}) copy-start(bf16[16,7,128,128]{3,2,1,0:T(8,128)(2,1)} %a.1) | copy-start | bytes 11010052
  15.7 2.9 %copy-start.1 = (bf16[16,128,128]{2,1,0:T(8,128)(2,1)S(1)}, bf16[16,128,128]{2,1,0:T(8,128)(2,1)}, u32[]{:S(2)}) copy-start(bf16[16,128,128]{2,1,0:T(8,128)(2,1)} %p.1) | copy-start | bytes 1572868
  23.4 12.0 %collective-permute-start.3 = (bf16[7,128,128]{2,1,0:T(8,128)(2,1)S(1)}, bf16[7,128,128]{2,1,0:T(8,128)(2,1)S(1)}, u32[]{:S(2)}, u32[]{:S(2)}) collective-permute-start(bf16[7,128,128]{2,1,0:T(8,128)(2,1)S(1)} %get-tuple-element.18), channel_id=1, source_target_pairs={{0,1},{1,2},{2,3},{3,4},{4,5},{5,6},{6,7},{7,8},{8,9},{9,10},{10,1... | collective-permute-start | bytes 688136 | tf_op jit(solution)/shard_map/ppermute | solution.py:275
  25.4 11.5 %collective-permute-start.4 = (bf16[7,128,128]{2,1,0:T(8,128)(2,1)S(1)}, bf16[7,128,128]{2,1,0:T(8,128)(2,1)S(1)}, u32[]{:S(2)}, u32[]{:S(2)}) collective-permute-start(bf16[7,128,128]{2,1,0:T(8,128)(2,1)S(1)} %get-tuple-element.19), channel_id=1, source_target_pairs={{1,0},{2,1},{3,2},{4,3},{5,4},{6,5},{7,6},{8,7},{9,8},{10,9},{11,1... | collective-permute-start | bytes 688136 | tf_op jit(solution)/shard_map/ppermute | solution.py:275

commit v6 on v5

--- a/solution.py
+++ b/solution.py
@@ -28,11 +28,12 @@
 
 
 def color_of(edge):
-    return 2 if edge % 128 in (119, 126) else edge % 2
+    return 2 if edge % 128 in (64, 119, 126) else edge % 2
 
 
 def color_in_kernel(edge):
-    return jnp.where(((edge & 127) == 126) | ((edge & 127) == 119), 2, edge & 1)
+    at = edge & 127
+    return jnp.where((at == 64) | (at == 119) | (at == 126), 2, at & 1)
 
 
 def dot(x, y):

time: 38.5 us -> 38.4 us (level)
  no operation moved by 1% of the time
where the time goes in v6:
time: 38.4 us; the launch traced here: 37.9 us
  starting transfers between devices  24.8 us (65%)
  Pallas kernels  9.96 us (26%)
  waiting for transfers between devices  2.23 us (6%)
  other arithmetic  0.75 us (2%)
    ppermute x1, starting transfers between devices, body(): from_1 = lax.ppermute(p_blocks, AXES, pairs[1])  10.8 us
    pallas_call x5, Pallas kernels, call(): pl.pallas_call(kernel, out_shape=outs, in_specs=[SMEM] * smems + [VMEM] *...  9.96 us
    ppermute x2, starting transfers between devices, body(): got = [lax.ppermute(msg_up, AXES, up), lax.ppermute(msg_down, AXES, down)]  9.9 us
    ppermute x1, starting transfers between devices, body(): from_0 = lax.ppermute(p_blocks, AXES, pairs[0])  3.47 us
    ppermute x2, waiting for transfers between devices, body(): got = [lax.ppermute(msg_up, AXES, up), lax.ppermute(msg_down, AXES, down)]  1.47 us
  transfers between devices with their start and end apart: 5, of which 2 were waited for; matrix products, arithmetic and copies ran while one was open for 2% of the time, Pallas kernels for 22%

profile of v6, /device:TPU:6, one launch (start us, length us, event | category | flops | bytes accessed | tf_op | source)
XLA Modules:
  0.0 37.9 jit_solution(5807173763969443057)
XLA Ops:
  0.0 3.5 %collective-permute-start = (bf16[16,128,128]{2,1,0:T(8,128)(2,1)}, bf16[16,128,128]{2,1,0:T(8,128)(2,1)S(1)}, u32[]{:S(2)}, u32[]{:S(2)}) collective-permute-start(bf16[16,128,128]{2,1,0:T(8,128)(2,1)} %p.1), channel_id=1, source_target_pairs={{0,1},{1,0},{2,3},{3,2},{4,5},{5,4},{6,7},{7,6},{8,9},{9,8},{10,11... | collective-permute-start | bytes 1572872 | tf_op jit(solution)/shard_map/ppermute | solution.py:267
  3.5 10.8 %collective-permute-start.1 = (bf16[16,128,128]{2,1,0:T(8,128)(2,1)}, bf16[16,128,128]{2,1,0:T(8,128)(2,1)S(1)}, u32[]{:S(2)}, u32[]{:S(2)}) collective-permute-start(bf16[16,128,128]{2,1,0:T(8,128)(2,1)} %p.1), channel_id=1, source_target_pairs={{1,2},{2,1},{3,4},{4,3},{5,6},{6,5},{7,8},{8,7},{9,10},{10,9},{11,... | collective-permute-start | bytes 1572872 | tf_op jit(solution)/shard_map/ppermute | solution.py:269
  14.3 0.7 %collective-permute-start.2 = (bf16[16,128,128]{2,1,0:T(8,128)(2,1)}, bf16[16,128,128]{2,1,0:T(8,128)(2,1)S(1)}, u32[]{:S(2)}, u32[]{:S(2)}) collective-permute-start(bf16[16,128,128]{2,1,0:T(8,128)(2,1)} %p.1), channel_id=1, source_target_pairs={{64,65},{65,64},{119,120},{120,119},{126,127},{127,126},{192,193},... | collective-permute-start | bytes 1572872 | tf_op jit(solution)/shard_map/ppermute | solution.py:270
  15.0 0.7 %pad_add_fusion.ints = s32[16,16]{1,0:T(8,128)S(1)} fusion(s32[1,16]{1,0:T(1,128)} %bitcast.6, s32[1,16]{1,0:T(1,128)} %bitcast.7, s32[7,16]{1,0:T(8,128)} %bitcast.4, s32[7,16]{1,0:T(8,128)} %bitcast.5), kind=kLoop, calls=%fused_computation | loop fusion | flops 768 | bytes 2048 | tf_op jit(solution)/shard_map/concatenate | solution.py:265
  15.7 0.0 copy-start
  15.7 0.0 copy-start.1
  15.7 2.9 %shard_map.64.table = s32[400]{0:T(512)S(1)} custom-call(s32[16,16]{1,0:T(8,128)S(1)} %pad_add_fusion.ints), custom_call_target="tpu_custom_call" | custom-call | flops 8589934592 | bytes 1048576 | tf_op jit(solution)/shard_map/pallas_call | solution.py:169
  18.6 0.0 copy-done
  18.7 0.0 copy-done.1
  18.7 3.3 %shard_map.65 = (f32[29,128,128]{2,1,0:T(8,128)S(1)}, f32[15,128,128]{2,1,0:T(8,128)S(1)}, bf16[72,128,128]{2,1,0:T(8,128)(2,1)S(1)}, bf16[24,128,128]{2,1,0:T(8,128)(2,1)S(1)}) custom-call(s32[400]{0:T(512)S(1)} %shard_map.64.table, bf16[16,7,128,128]{3,2,1,0:T(8,128)(2,1)S(1)} %copy-done, bf16[16,128,128]{2,1,0:T(8,128)(2,1)S(1)} %copy-done.1), custom_call_target="tpu_custom_call" | custom-call | flops 536870912 | bytes 8388608 | tf_op jit(solution)/shard_map/pallas_call | solution.py:169
  22.0 0.0 collective-permute-done.from_0
  22.0 0.7 %collective-permute-done.1.from_1 = bf16[16,128,128]{2,1,0:T(8,128)(2,1)S(1)} collective-permute-done((bf16[16,128,128]{2,1,0:T(8,128)(2,1)}, bf16[16,128,128]{2,1,0:T(8,128)(2,1)S(1)}, u32[]{:S(2)}, u32[]{:S(2)}) %collective-permute-start.1) | collective-permute-done | bytes 524320 | tf_op jit(solution)/shard_map/ppermute | solution.py:269
  22.7 0.0 collective-permute-done.2.from_2
  22.7 0.9 %shard_map.67 = (bf16[7,128,128]{2,1,0:T(8,128)(2,1)S(1)}, bf16[7,128,128]{2,1,0:T(8,128)(2,1)S(1)}) custom-call(s32[400]{0:T(512)S(1)} %shard_map.64.table, f32[15,128,128]{2,1,0:T(8,128)S(1)} %get-tuple-element.16.edge_acc, bf16[24,128,128]{2,1,0:T(8,128)(2,1)S(1)} %get-tuple-element.17.left_edge, bf16[16,128,128]{2,1,0:T(8,128)(2,1)S(1)} %collective-permute-done.from_0, ...), custom_call_target="tpu_custom_call" | custom-call | flops 33554432 | bytes 2097152 | tf_op jit(solution)/shard_map/pallas_call | solution.py:169
  23.6 1.9 %collective-permute-start.3 = (bf16[7,128,128]{2,1,0:T(8,128)(2,1)S(1)}, bf16[7,128,128]{2,1,0:T(8,128)(2,1)S(1)}, u32[]{:S(2)}, u32[]{:S(2)}) collective-permute-start(bf16[7,128,128]{2,1,0:T(8,128)(2,1)S(1)} %get-tuple-element.18), channel_id=1, source_target_pairs={{0,1},{1,2},{2,3},{3,4},{4,5},{5,6},{6,7},{7,8},{8,9},{9,10},{10,1... | collective-permute-start | bytes 688136 | tf_op jit(solution)/shard_map/ppermute | solution.py:276
  25.6 8.0 %collective-permute-start.4 = (bf16[7,128,128]{2,1,0:T(8,128)(2,1)S(1)}, bf16[7,128,128]{2,1,0:T(8,128)(2,1)S(1)}, u32[]{:S(2)}, u32[]{:S(2)}) collective-permute-start(bf16[7,128,128]{2,1,0:T(8,128)(2,1)S(1)} %get-tuple-element.19), channel_id=1, source_target_pairs={{1,0},{2,1},{3,2},{4,3},{5,4},{6,5},{7,6},{8,7},{9,8},{10,9},{11,1... | collective-permute-start | bytes 688136 | tf_op jit(solution)/shard_map/ppermute | solution.py:276
  33.5 2.0 %shard_map.66 = (f32[14,128,128]{2,1,0:T(8,128)S(1)}, bf16[4,7,128,128]{3,2,1,0:T(8,128)(2,1)}) custom-call(s32[400]{0:T(512)S(1)} %shard_map.64.table, f32[29,128,128]{2,1,0:T(8,128)S(1)} %get-tuple-element.13.acc_in, bf16[72,128,128]{2,1,0:T(8,128)(2,1)S(1)} %get-tuple-element.14.left_halo, bf16[16,128,128]{2,1,0:T(8,128)(2,1)S(1)} %collective-permute-done.from_0, ...), custom_call_target="tpu_custom_call" | custom-call | flops 134217728 | bytes 6291456 | tf_op jit(solution)/shard_map/pallas_call | solution.py:169
  35.6 0.0 collective-permute-done.3.from_before
  35.6 1.5 %collective-permute-done.4.from_after = bf16[7,128,128]{2,1,0:T(8,128)(2,1)S(1)} collective-permute-done((bf16[7,128,128]{2,1,0:T(8,128)(2,1)S(1)}, bf16[7,128,128]{2,1,0:T(8,128)(2,1)S(1)}, u32[]{:S(2)}, u32[]{:S(2)}) %collective-permute-start.4) | collective-permute-done | bytes 229408 | tf_op jit(solution)/shard_map/ppermute | solution.py:276
  37.1 0.8 %shard_map.68 = bf16[4,7,128,128]{3,2,1,0:T(8,128)(2,1)} custom-call(f32[14,128,128]{2,1,0:T(8,128)S(1)} %get-tuple-element.15.acc, bf16[7,128,128]{2,1,0:T(8,128)(2,1)S(1)} %collective-permute-done.3.from_before, bf16[7,128,128]{2,1,0:T(8,128)(2,1)S(1)} %collective-permute-done.4.from_after, ...), custom_call_target="tpu_custom_call", output_to_operand_aliasing={{}: (3, {})} | custom-call | flops 4194304 | bytes 2097152 | tf_op jit(solution)/shard_map/pallas_call | solution.py:169
Async XLA Ops:
  0.0 22.0 %collective-permute-start = (bf16[16,128,128]{2,1,0:T(8,128)(2,1)}, bf16[16,128,128]{2,1,0:T(8,128)(2,1)S(1)}, u32[]{:S(2)}, u32[]{:S(2)}) collective-permute-start(bf16[16,128,128]{2,1,0:T(8,128)(2,1)} %p.1), channel_id=1, source_target_pairs={{0,1},{1,0},{2,3},{3,2},{4,5},{5,4},{6,7},{7,6},{8,9},{9,8},{10,11... | collective-permute-start | bytes 1572872 | tf_op jit(solution)/shard_map/ppermute | solution.py:267
  3.5 19.3 %collective-permute-start.1 = (bf16[16,128,128]{2,1,0:T(8,128)(2,1)}, bf16[16,128,128]{2,1,0:T(8,128)(2,1)S(1)}, u32[]{:S(2)}, u32[]{:S(2)}) collective-permute-start(bf16[16,128,128]{2,1,0:T(8,128)(2,1)} %p.1), channel_id=1, source_target_pairs={{1,2},{2,1},{3,4},{4,3},{5,6},{6,5},{7,8},{8,7},{9,10},{10,9},{11,... | collective-permute-start | bytes 1572872 | tf_op jit(solution)/shard_map/ppermute | solution.py:269
  14.3 8.5 %collective-permute-start.2 = (bf16[16,128,128]{2,1,0:T(8,128)(2,1)}, bf16[16,128,128]{2,1,0:T(8,128)(2,1)S(1)}, u32[]{:S(2)}, u32[]{:S(2)}) collective-permute-start(bf16[16,128,128]{2,1,0:T(8,128)(2,1)} %p.1), channel_id=1, source_target_pairs={{64,65},{65,64},{119,120},{120,119},{126,127},{127,126},{192,193},... | collective-permute-start | bytes 1572872 | tf_op jit(solution)/shard_map/ppermute | solution.py:270
  15.7 2.9 %copy-start = (bf16[16,7,128,128]{3,2,1,0:T(8,128)(2,1)S(1)}, bf16[16,7,128,128]{3,2,1,0:T(8,128)(2,1)}, u32[]{:S(2)}) copy-start(bf16[16,7,128,128]{3,2,1,0:T(8,128)(2,1)} %a.1) | copy-start | bytes 11010052
  15.7 2.9 %copy-start.1 = (bf16[16,128,128]{2,1,0:T(8,128)(2,1)S(1)}, bf16[16,128,128]{2,1,0:T(8,128)(2,1)}, u32[]{:S(2)}) copy-start(bf16[16,128,128]{2,1,0:T(8,128)(2,1)} %p.1) | copy-start | bytes 1572868
  23.6 12.0 %collective-permute-start.3 = (bf16[7,128,128]{2,1,0:T(8,128)(2,1)S(1)}, bf16[7,128,128]{2,1,0:T(8,128)(2,1)S(1)}, u32[]{:S(2)}, u32[]{:S(2)}) collective-permute-start(bf16[7,128,128]{2,1,0:T(8,128)(2,1)S(1)} %get-tuple-element.18), channel_id=1, source_target_pairs={{0,1},{1,2},{2,3},{3,4},{4,5},{5,6},{6,7},{7,8},{8,9},{9,10},{10,1... | collective-permute-start | bytes 688136 | tf_op jit(solution)/shard_map/ppermute | solution.py:276
  25.6 11.5 %collective-permute-start.4 = (bf16[7,128,128]{2,1,0:T(8,128)(2,1)S(1)}, bf16[7,128,128]{2,1,0:T(8,128)(2,1)S(1)}, u32[]{:S(2)}, u32[]{:S(2)}) collective-permute-start(bf16[7,128,128]{2,1,0:T(8,128)(2,1)S(1)} %get-tuple-element.19), channel_id=1, source_target_pairs={{1,0},{2,1},{3,2},{4,3},{5,4},{6,5},{7,6},{8,7},{9,8},{10,9},{11,1... | collective-permute-start | bytes 688136 | tf_op jit(solution)/shard_map/ppermute | solution.py:276
